TPU v7x, 32 devices: a whole 2x2x4 slice. The times are simulated.
32 devices in a mesh: shard: 4 (over y, x), replica: 8 (over z, core).
Axes of the slice: x: 2, y: 2, z: 4, core: 2. Of those that a mesh axis runs over, the one named last changes fastest.
Arguments:
- tokens: bfloat16 [6304, 768], P(('shard', 'replica')), may hold values from -6 to 6
- ln_gain: bfloat16 [2, 2, 768], P(None, None, 'shard'), may hold values from 0.25 to 1.75
- ln_bias: bfloat16 [2, 2, 768], P(None, None, 'shard'), may hold values from -1.796875 to 1.796875
- w_qkv: bfloat16 [2, 768, 2304], P(None, 'shard'), may hold values from -0.21875 to 0.21875
- w_proj: bfloat16 [2, 768, 768], P(None, 'shard'), may hold values from -1.5 to 1.5
- w_router: bfloat16 [2, 768, 3], P(None, 'shard'), may hold values from -0.21875 to 0.21875
- expert_in: bfloat16 [2, 3, 3072, 768], P(None, None, 'shard'), may hold values from -0.21875 to 0.21875
- expert_out: bfloat16 [2, 3, 3072, 768], P(None, None, 'shard'), may hold values from -0.21875 to 0.21875
- image_count: int32 [32], P(('shard', 'replica')), may hold values from 0 to 1, as said below
- expert_ids: int32 [2, 6304, 2], P(None, ('shard', 'replica')), may hold values from 0 to 2, as said below
- slot_index: int32 [2, 6304, 2], P(None, ('shard', 'replica')), may hold values from -1 to 130, as said below
- cotangent: bfloat16 [6304, 768], P(('shard', 'replica')), may hold values from -6 to 6
Outputs:
- mixed: bfloat16 [6304, 768], P(('shard', 'replica'))
- grad_tokens: float32 [6304, 768], P(('shard', 'replica'))
- grad_gain: float32 [2, 2, 768], P(None, None, 'shard')
- grad_bias: float32 [2, 768], P(None, 'shard')
- grad_bias_second: float32 [2, 768], P(None, 'shard')
- grad_qkv: float32 [2, 768, 2304], P(None, 'shard')
- grad_proj: float32 [2, 768, 768], P(None, 'shard')
- grad_router: float32 [2, 768, 3], P(None, 'shard')
- grad_expert_in: float32 [2, 3, 3072, 768], P(None, None, 'shard')
- grad_expert_out: float32 [2, 3, 3072, 768], P(None, None, 'shard')
Inputs may be any that keep to these rules, and one draw needn't show every extreme that they name: `image_count`: images present on a device fill its first image slots; some device has all 1 present. `expert_ids`: the two experts of a token differ. `slot_index`: on one device and in one block the positions taken in an expert's buffer are distinct and run from 0 up without gaps; -1 marks a dropped choice, and both choices of every row of an absent image are -1.
All inputs are finite; a program needn't handle non-finite values.
Results may differ from a plain program's by a relative error of at most 0.018.
Values may be sent and summed in bfloat16 or wider, within the bound.
A program may use at most 256 MiB of HBM per device.

v0:
```python
import jax
import jax.numpy as jnp
from jax import lax
from jax.sharding import PartitionSpec as P

HEADS = 12
HEAD_DIM = 64
SEQ = 197


precise = lax.Precision.HIGHEST


def norm_forward(values, gain, bias):
    centre = values - jnp.mean(values, axis=-1, keepdims=True)
    spread = jnp.mean(centre * centre, axis=-1, keepdims=True)
    scaled = lax.rsqrt(spread + 1e-06)
    normal = centre * scaled
    return (normal * gain + bias, normal, scaled)


def norm_backward(upstream, gain, normal, scaled):
    inner = upstream * gain
    centred = inner - jnp.mean(inner, axis=-1, keepdims=True)
    result = scaled * (centred - normal * jnp.mean(inner * normal, axis=-1, keepdims=True))
    return (result, jnp.sum(upstream * normal, axis=0), jnp.sum(upstream, axis=0))


def gelu_slope(values):
    return (
        0.5 * (1.0 + lax.erf(values * 0.7071067811865476))
        + values * jnp.exp(-0.5 * values * values) * 0.3989422804014327
    )


def split_heads(packed):
    images = packed.shape[0] // SEQ
    blocks = packed.reshape(images, SEQ, 3, HEADS, HEAD_DIM)
    return (blocks[:, :, 0], blocks[:, :, 1], blocks[:, :, 2])


def head_scores(queries, key_rows):
    return (
        jnp.einsum("bqhd,bkhd->bhqk", queries, key_rows, preferred_element_type=jnp.float32) * 0.125
    )


def attend(packed):
    queries, key_rows, val_rows = split_heads(packed)
    scores = head_scores(queries, key_rows)
    log_total = jax.nn.logsumexp(scores, axis=-1, keepdims=True)
    weights = jnp.exp(scores - log_total).astype(jnp.bfloat16)
    result = jnp.einsum("bhqk,bkhd->bqhd", weights, val_rows, preferred_element_type=jnp.float32)
    return (result.astype(jnp.bfloat16).reshape(packed.shape[0], HEADS * HEAD_DIM), log_total)


def attend_back(packed, log_total, upstream):
    queries, key_rows, val_rows = split_heads(packed)
    weights = jnp.exp(head_scores(queries, key_rows) - log_total)
    incoming = upstream.reshape(queries.shape)
    grad_values = jnp.einsum(
        "bhqk,bqhd->bkhd",
        weights.astype(jnp.bfloat16),
        incoming,
        preferred_element_type=jnp.float32,
    )
    grad_weights = jnp.einsum(
        "bqhd,bkhd->bhqk", incoming, val_rows, preferred_element_type=jnp.float32
    )
    inner = jnp.sum(weights * grad_weights, axis=-1, keepdims=True)
    grad_scores = (weights * (grad_weights - inner)).astype(jnp.bfloat16)
    grad_queries = (
        jnp.einsum("bhqk,bkhd->bqhd", grad_scores, key_rows, preferred_element_type=jnp.float32)
        * 0.125
    )
    grad_keys = (
        jnp.einsum("bhqk,bqhd->bkhd", grad_scores, queries, preferred_element_type=jnp.float32)
        * 0.125
    )
    stacked = jnp.stack([grad_queries, grad_keys, grad_values], axis=2)
    return stacked.astype(jnp.bfloat16).reshape(packed.shape)


def body(
    tokens,
    ln_gain,
    ln_bias,
    w_qkv,
    w_proj,
    w_router,
    expert_in,
    expert_out,
    image_count,
    expert_ids,
    slot_index,
    cotangent,
):
    rows = tokens.shape[0]
    width = tokens.shape[1]
    layers = w_qkv.shape[0]
    experts = expert_in.shape[1]
    capacity = 2 * rows // experts
    live = (jnp.arange(rows, dtype=jnp.int32) // SEQ < image_count[0]).astype(jnp.float32)[:, None]
    positions = jnp.arange(experts * capacity, dtype=jnp.int32)
    state = tokens.astype(jnp.float32)
    saved = []
    kept_weights = []
    for layer_idx in range(layers):
        gathered = (
            lax.all_gather(ln_gain[layer_idx], "shard", axis=1, tiled=True),
            lax.all_gather(ln_bias[layer_idx], "shard", axis=1, tiled=True),
            lax.all_gather(w_qkv[layer_idx], "shard", axis=0, tiled=True),
            lax.all_gather(w_proj[layer_idx], "shard", axis=0, tiled=True),
            lax.all_gather(w_router[layer_idx], "shard", axis=0, tiled=True),
        )
        kept_weights.append(gathered)
        gain = gathered[0].astype(jnp.float32)
        bias = gathered[1].astype(jnp.float32)
        first_out, first_normal, first_scaled = norm_forward(state, gain[0], bias[0])
        first_low = first_out.astype(jnp.bfloat16)
        packed = jnp.dot(first_low, gathered[2], preferred_element_type=jnp.float32).astype(
            jnp.bfloat16
        )
        attended, log_total = attend(packed)
        after = state + jnp.dot(attended, gathered[3], preferred_element_type=jnp.float32)
        second_out, second_normal, second_scaled = norm_forward(after, gain[1], bias[1])
        second_low = second_out.astype(jnp.bfloat16)
        logits = jnp.dot(second_low, gathered[4], preferred_element_type=jnp.float32)
        probs = jax.nn.softmax(logits, axis=-1)
        routes = expert_ids[layer_idx]
        places = slot_index[layer_idx]
        valid = places >= 0
        flat_index = routes * capacity + jnp.where(valid, places, 0)
        table = jnp.sum(
            ((positions[:, None, None] == flat_index[None]) & valid[None]).astype(jnp.bfloat16),
            axis=2,
        )
        dispatched = jnp.dot(table, second_low, preferred_element_type=jnp.float32).astype(
            jnp.bfloat16
        )
        dispatched = dispatched.reshape(experts, capacity, width)
        group_rows = lax.all_gather(dispatched, "shard", axis=1, tiled=True)
        before_all = jnp.einsum(
            "ecd,efd->ecf", group_rows, expert_in[layer_idx], preferred_element_type=jnp.float32
        )
        hidden = jax.nn.gelu(before_all, approximate=False).astype(jnp.bfloat16)
        partial_rows = jnp.einsum(
            "ecf,efd->ecd", hidden, expert_out[layer_idx], preferred_element_type=jnp.float32
        )
        returned = lax.psum_scatter(
            partial_rows.astype(jnp.bfloat16), "shard", scatter_dimension=1, tiled=True
        ).astype(jnp.float32)
        gates = jnp.take_along_axis(probs, routes, axis=1) * valid.astype(jnp.float32)
        picked = returned.reshape(experts * capacity, width)[flat_index]
        saved.append(
            (
                first_normal,
                first_scaled,
                first_low,
                packed,
                attended,
                log_total,
                second_normal,
                second_scaled,
                second_low,
                probs,
                flat_index,
                valid,
                gates,
                picked,
                group_rows,
                before_all,
                routes,
            )
        )
        state = after + jnp.sum(gates[:, :, None] * picked, axis=1)
    mixed = (state * live).astype(jnp.bfloat16)
    grad_state = cotangent.astype(jnp.float32) * live
    block_lists = [None] * layers
    expert_lists = [None] * layers
    for layer_idx in reversed(range(layers)):
        (
            first_normal,
            first_scaled,
            first_low,
            packed,
            attended,
            log_total,
            second_normal,
            second_scaled,
            second_low,
            probs,
            flat_index,
            valid,
            gates,
            picked,
            group_rows,
            before_all,
            routes,
        ) = saved[layer_idx]
        gathered = (
            lax.all_gather(ln_gain[layer_idx], "shard", axis=1, tiled=True),
            lax.all_gather(ln_bias[layer_idx], "shard", axis=1, tiled=True),
            lax.all_gather(w_qkv[layer_idx], "shard", axis=0, tiled=True),
            lax.all_gather(w_proj[layer_idx], "shard", axis=0, tiled=True),
            lax.all_gather(w_router[layer_idx], "shard", axis=0, tiled=True),
        )
        gain = gathered[0].astype(jnp.float32)
        valid_float = valid.astype(jnp.float32)
        grad_gates = jnp.sum(grad_state[:, None, :] * picked, axis=-1) * valid_float
        target = jnp.where(valid, flat_index, experts * capacity).reshape(-1)
        shares = (gates[:, :, None] * grad_state[:, None, :]).reshape(-1, width)
        grad_returned = (
            jnp.zeros((experts * capacity, width), jnp.float32).at[target].add(shares, mode="drop")
        )
        grad_returned = grad_returned.astype(jnp.bfloat16).reshape(experts, capacity, width)
        group_grad = lax.all_gather(grad_returned, "shard", axis=1, tiled=True)
        hidden = jax.nn.gelu(before_all, approximate=False).astype(jnp.bfloat16)
        grad_hidden = jnp.einsum(
            "ecd,efd->ecf", group_grad, expert_out[layer_idx], preferred_element_type=jnp.float32
        )
        grad_before = (grad_hidden * gelu_slope(before_all)).astype(jnp.bfloat16)
        grad_out = jnp.einsum(
            "ecf,ecd->efd", hidden, group_grad, preferred_element_type=jnp.float32
        )
        grad_in = jnp.einsum(
            "ecf,ecd->efd", grad_before, group_rows, preferred_element_type=jnp.float32
        )
        row_terms = jnp.einsum(
            "ecf,efd->ecd", grad_before, expert_in[layer_idx], preferred_element_type=jnp.float32
        )
        grad_rows = lax.psum_scatter(
            row_terms.astype(jnp.bfloat16), "shard", scatter_dimension=1, tiled=True
        ).astype(jnp.float32)
        owned_in, owned_out = (
            lax.psum_scatter(
                grad_in.astype(jnp.bfloat16), "replica", scatter_dimension=1, tiled=True
            ).astype(jnp.float32),
            lax.psum_scatter(
                grad_out.astype(jnp.bfloat16), "replica", scatter_dimension=1, tiled=True
            ).astype(jnp.float32),
        )
        expert_lists[layer_idx] = (owned_in, owned_out)
        choice_hits = (
            routes[:, :, None] == jnp.arange(experts, dtype=jnp.int32)[None, None, :]
        ).astype(jnp.float32)
        grad_probs = jnp.sum(grad_gates[:, :, None] * choice_hits, axis=1)
        grad_logits = probs * (grad_probs - jnp.sum(probs * grad_probs, axis=-1, keepdims=True))
        router_wide = gathered[4].astype(jnp.float32)
        grad_router = jnp.dot(second_low.astype(jnp.float32).T, grad_logits, precision=precise)
        routed_back = grad_rows.reshape(experts * capacity, width)[flat_index]
        grad_second = jnp.sum(routed_back * valid_float[:, :, None], axis=1)
        grad_second = grad_second + jnp.dot(grad_logits, router_wide.T, precision=precise)
        norm_part, gain_second, bias_second = norm_backward(
            grad_second, gain[1], second_normal, second_scaled
        )
        grad_after = grad_state + norm_part
        grad_proj_in = grad_after.astype(jnp.bfloat16)
        grad_proj = jnp.dot(attended.T, grad_proj_in, preferred_element_type=jnp.float32)
        grad_attended = jnp.dot(
            grad_proj_in, gathered[3].T, preferred_element_type=jnp.float32
        ).astype(jnp.bfloat16)
        grad_packed = attend_back(packed, log_total, grad_attended)
        grad_qkv = jnp.dot(first_low.T, grad_packed, preferred_element_type=jnp.float32)
        grad_first = jnp.dot(grad_packed, gathered[2].T, preferred_element_type=jnp.float32)
        norm_first, gain_first, bias_first = norm_backward(
            grad_first, gain[0], first_normal, first_scaled
        )
        grad_state = grad_after + norm_first
        block_terms = (
            jnp.stack([gain_first, gain_second]),
            jnp.stack([bias_first, bias_second]),
            grad_qkv,
            grad_proj,
            grad_router,
        )
        block_lists[layer_idx] = (
            lax.psum_scatter(block_terms[0], ("shard", "replica"), scatter_dimension=1, tiled=True),
            lax.psum_scatter(block_terms[1], ("shard", "replica"), scatter_dimension=1, tiled=True),
            lax.psum_scatter(block_terms[2], ("shard", "replica"), scatter_dimension=0, tiled=True),
            lax.psum_scatter(block_terms[3], ("shard", "replica"), scatter_dimension=0, tiled=True),
            lax.psum_scatter(block_terms[4], ("shard", "replica"), scatter_dimension=0, tiled=True),
        )
    collected = (
        jnp.stack([item[0] for item in block_lists]),
        jnp.stack([item[1] for item in block_lists]),
        jnp.stack([item[2] for item in block_lists]),
        jnp.stack([item[3] for item in block_lists]),
        jnp.stack([item[4] for item in block_lists]),
        jnp.stack([item[0] for item in expert_lists]),
        jnp.stack([item[1] for item in expert_lists]),
    )
    final = (
        lax.all_gather(collected[0].astype(jnp.bfloat16), "replica", axis=2, tiled=True).astype(
            jnp.float32
        ),
        lax.all_gather(collected[1].astype(jnp.bfloat16), "replica", axis=2, tiled=True).astype(
            jnp.float32
        ),
        lax.all_gather(collected[2].astype(jnp.bfloat16), "replica", axis=1, tiled=True).astype(
            jnp.float32
        ),
        lax.all_gather(collected[3].astype(jnp.bfloat16), "replica", axis=1, tiled=True).astype(
            jnp.float32
        ),
        lax.all_gather(collected[4].astype(jnp.bfloat16), "replica", axis=1, tiled=True).astype(
            jnp.float32
        ),
        lax.all_gather(collected[5].astype(jnp.bfloat16), "replica", axis=2, tiled=True).astype(
            jnp.float32
        ),
        lax.all_gather(collected[6].astype(jnp.bfloat16), "replica", axis=2, tiled=True).astype(
            jnp.float32
        ),
    )
    return (
        mixed,
        grad_state,
        final[0],
        final[1][:, 0],
        final[1][:, 1],
        final[2],
        final[3],
        final[4],
        final[5],
        final[6],
    )


def solution(mesh):
    placed = (
        P(("shard", "replica"), None),
        P(None, None, "shard"),
        P(None, None, "shard"),
        P(None, "shard", None),
        P(None, "shard", None),
        P(None, "shard", None),
        P(None, None, "shard", None),
        P(None, None, "shard", None),
        P(("shard", "replica")),
        P(None, ("shard", "replica"), None),
        P(None, ("shard", "replica"), None),
        P(("shard", "replica"), None),
    )
    return jax.shard_map(
        body,
        mesh=mesh,
        in_specs=placed,
        out_specs=(
            P(("shard", "replica"), None),
            P(("shard", "replica"), None),
            P(None, None, "shard"),
            P(None, "shard"),
            P(None, "shard"),
            P(None, "shard", None),
            P(None, "shard", None),
            P(None, "shard", None),
            P(None, None, "shard", None),
            P(None, None, "shard", None),
        ),
        check_vma=False,
    )
```

profile of v0, /device:TPU:0, one launch (start us, length us, event | category | flops | bytes accessed | tf_op | source)
XLA Modules:
  0.0 1566.0 jit_solution(8264528837691743064)
XLA Ops:
  48.5 13.4 all-gather.36.cloned.1.call-done
  68.2 23.9 %all-gather.38.cloned.1.call-done = bf16[1,768,768]{2,1,0:T(8,128)(2,1)} async-done(((bf16[1,192,768]{2,1,0:T(8,128)(2,1)}), bf16[1,768,768]{2,1,0:T(8,128)(2,1)}) %all-gather.38.cloned.1.call-update) | async-done | bytes 1179664 | tf_op jit(solution)/shard_map/all_gather | solution.py:113
  96.7 44.1 %all-gather.22.cloned.1.call-done = bf16[3,524,768]{2,0,1:T(4,128)(2,1)} async-done(((bf16[3,131,768]{2,0,1:T(4,128)(2,1)}), bf16[3,524,768]{2,0,1:T(4,128)(2,1)}) %all-gather.22.cloned.1.call-update) | async-done | bytes 2414608 | tf_op jit(solution)/shard_map/all_gather | solution.py:142
  224.4 24.6 %all-reduce.16.cloned.1.call-done = bf16[3,524,768]{2,1,0:T(8,128)(2,1)} async-done(((bf16[3,524,768]{2,1,0:T(8,128)(2,1)}), bf16[3,524,768]{2,1,0:T(8,128)(2,1)}) %all-reduce.16.cloned.1.call-update) | async-done | bytes 2414608
  259.2 39.7 %all-gather.40.cloned.1.call-done = bf16[1,768,2304]{2,1,0:T(8,128)(2,1)} async-done(((bf16[1,192,2304]{2,1,0:T(8,128)(2,1)}), bf16[1,768,2304]{2,1,0:T(8,128)(2,1)}) %all-gather.40.cloned.1.call-update) | async-done | bytes 3538960 | tf_op jit(solution)/shard_map/all_gather | solution.py:112
  308.0 20.9 %all-gather.42.cloned.1.call-done = bf16[1,768,768]{2,1,0:T(8,128)(2,1)} async-done(((bf16[1,192,768]{2,1,0:T(8,128)(2,1)}), bf16[1,768,768]{2,1,0:T(8,128)(2,1)}) %all-gather.42.cloned.1.call-update) | async-done | bytes 1179664 | tf_op jit(solution)/shard_map/all_gather | solution.py:113
  402.8 22.0 %all-gather.26.cloned.1.call-done = bf16[3,524,768]{2,0,1:T(4,128)(2,1)} async-done(((bf16[3,131,768]{2,0,1:T(4,128)(2,1)}), bf16[3,524,768]{2,0,1:T(4,128)(2,1)}) %all-gather.26.cloned.1.call-update) | async-done | bytes 2414608 | tf_op jit(solution)/shard_map/all_gather | solution.py:217
  441.6 113.2 %all-reduce.20.cloned.1.call-done = (bf16[3,524,768]{2,1,0:T(8,128)(2,1)}, bf16[3,524,768]{2,1,0:T(8,128)(2,1)}) async-done(((bf16[3,524,768]{2,1,0:T(8,128)(2,1)}, bf16[3,524,768]{2,1,0:T(8,128)(2,1)}), (bf16[3,524,768]{2,1,0:T(8,128)(2,1)}, bf16[3,524,768]{2,1,0:T(8,128)(2,1)})) %all-reduce.20.cloned.1.call-update) | async-done | bytes 4829200
  603.6 45.2 %all-gather.28.cloned.1.call-done = bf16[3,524,768]{2,0,1:T(4,128)(2,1)} async-done(((bf16[3,131,768]{2,0,1:T(4,128)(2,1)}), bf16[3,524,768]{2,0,1:T(4,128)(2,1)}) %all-gather.28.cloned.1.call-update) | async-done | bytes 2414608 | tf_op jit(solution)/shard_map/all_gather | solution.py:217
  670.9 67.7 %all-reduce.18.cloned.1.call-done = bf16[3,524,768]{2,1,0:T(8,128)(2,1)} async-done(((bf16[3,524,768]{2,1,0:T(8,128)(2,1)}), bf16[3,524,768]{2,1,0:T(8,128)(2,1)}) %all-reduce.18.cloned.1.call-update) | async-done | bytes 2414608
  792.8 71.3 %reduce-scatter.21.cloned.1.call-done = f32[24,2304]{1,0:T(8,128)} async-done(((f32[768,2304]{1,0:T(8,128)}), f32[24,2304]{1,0:T(8,128)}) %reduce-scatter.21.cloned.1.call-update) | async-done | bytes 221200 | tf_op jit(solution)/shard_map/reduce_scatter | solution.py:280
  865.1 124.6 %reduce-scatter.19.cloned.1.call-done = f32[24,2304]{1,0:T(8,128)} async-done(((f32[768,2304]{1,0:T(8,128)}), f32[24,2304]{1,0:T(8,128)}) %reduce-scatter.19.cloned.1.call-update) | async-done | bytes 221200 | tf_op jit(solution)/shard_map/reduce_scatter | solution.py:280
  991.5 44.2 %reduce-scatter.29.cloned.1.call-done = bf16[3,96,768]{2,1,0:T(8,128)(2,1)} async-done(((bf16[3,768,768]{2,1,0:T(8,128)(2,1)}), bf16[3,96,768]{2,1,0:T(8,128)(2,1)}) %reduce-scatter.29.cloned.1.call-update) | async-done | bytes 442384 | tf_op jit(solution)/shard_map/reduce_scatter | solution.py:236
  1035.7 44.6 %reduce-scatter.27.cloned.1.call-done = bf16[3,96,768]{2,1,0:T(8,128)(2,1)} async-done(((bf16[3,768,768]{2,1,0:T(8,128)(2,1)}), bf16[3,96,768]{2,1,0:T(8,128)(2,1)}) %reduce-scatter.27.cloned.1.call-update) | async-done | bytes 442384 | tf_op jit(solution)/shard_map/reduce_scatter | solution.py:236
  1082.5 42.3 %reduce-scatter.33.cloned.1.call-done = bf16[3,96,768]{2,1,0:T(8,128)(2,1)} async-done(((bf16[3,768,768]{2,1,0:T(8,128)(2,1)}), bf16[3,96,768]{2,1,0:T(8,128)(2,1)}) %reduce-scatter.33.cloned.1.call-update) | async-done | bytes 442384 | tf_op jit(solution)/shard_map/reduce_scatter | solution.py:239
  1124.8 44.6 %reduce-scatter.31.cloned.1.call-done = bf16[3,96,768]{2,1,0:T(8,128)(2,1)} async-done(((bf16[3,768,768]{2,1,0:T(8,128)(2,1)}), bf16[3,96,768]{2,1,0:T(8,128)(2,1)}) %reduce-scatter.31.cloned.1.call-update) | async-done | bytes 442384 | tf_op jit(solution)/shard_map/reduce_scatter | solution.py:239
  1172.3 99.9 %reduce-scatter.25.cloned.1.call-done = f32[24,768]{1,0:T(8,128)} async-done(((f32[768,768]{1,0:T(8,128)}), f32[24,768]{1,0:T(8,128)}) %reduce-scatter.25.cloned.1.call-update) | async-done | bytes 73744 | tf_op jit(solution)/shard_map/reduce_scatter | solution.py:281
  1276.7 41.1 %all-reduce.10 = (bf16[2,768]{1,0:T(2,128)(2,1)S(1)}, bf16[2,768]{1,0:T(2,128)(2,1)S(1)}, bf16[2,768]{1,0:T(2,128)(2,1)S(1)}, bf16[2,768]{1,0:T(2,128)(2,1)S(1)}...) all-reduce(f32[2,768]{1,0:T(2,128)S(1)} %pad_maximum_fusion.7, ...), channel_id=17, replica_groups=mesh['shard'=4,'replica'=8] {'shard','replica'}, use_global_device_ids=true, to_apply=%region_49.51.clone | all-reduce | flops 10752 | bytes 64512
  1318.6 14.0 all_gather.85
  1333.3 13.9 all_gather.89
  1347.9 13.9 all_gather.86
  1377.3 16.1 %all_gather.88 = bf16[2,192,768]{2,1,0:T(8,128)(2,1)S(1)} all-gather(bf16[2,24,768]{2,1,0:T(8,128)(2,1)S(1)} %pad_maximum_fusion.5), channel_id=1, replica_groups=mesh['shard'=4,'replica'=8] {'replica'}, dimensions={1}, use_global_device_ids=true | all-gather | bytes 663552 | tf_op jit(solution)/shard_map/all_gather | solution.py:303
  1408.7 69.3 %all-gather.32.cloned.1.call-done = bf16[2,3,768,768]{3,2,1,0:T(8,128)(2,1)} async-done(((bf16[2,3,96,768]{3,2,1,0:T(8,128)(2,1)}), bf16[2,3,768,768]{3,2,1,0:T(8,128)(2,1)}) %all-gather.32.cloned.1.call-update) | async-done | bytes 7077904 | tf_op jit(solution)/shard_map/all_gather | solution.py:309
  1488.1 61.3 %all-gather.34.cloned.1.call-done = bf16[2,3,768,768]{3,2,1,0:T(8,128)(2,1)} async-done(((bf16[2,3,96,768]{3,2,1,0:T(8,128)(2,1)}), bf16[2,3,768,768]{3,2,1,0:T(8,128)(2,1)}) %all-gather.34.cloned.1.call-update) | async-done | bytes 7077904 | tf_op jit(solution)/shard_map/all_gather | solution.py:312
  (530 shorter events, 432.0 us)
Async XLA Ops:
  7.2 54.7 %all-gather.36.cloned.1.call-start = ((), (), s32[]{:S(2)}) async-start(), calls=%async_computation.23 | async-start | bytes 4423680 | tf_op jit(solution)/shard_map/all_gather | solution.py:112
  10.1 82.0 %all-gather.38.cloned.1.call-start = ((), (), s32[]{:S(2)}) async-start(), calls=%async_computation.24 | async-start | bytes 1474560 | tf_op jit(solution)/shard_map/all_gather | solution.py:113
  11.1 129.8 %all-gather.22.cloned.1.call-start = ((), (), s32[]{:S(2)}) async-start(), calls=%async_computation.8 | async-start | bytes 4024320 | tf_op jit(solution)/shard_map/all_gather | solution.py:142
  96.1 152.9 %all-reduce.16.cloned.1.call-start = ((), (), s32[]{:S(2)}) async-start(), calls=%async_computation.27 | async-start | bytes 4866048
  165.2 133.6 %all-gather.40.cloned.1.call-start = ((), (), s32[]{:S(2)}) async-start(), calls=%async_computation.25 | async-start | bytes 4423680 | tf_op jit(solution)/shard_map/all_gather | solution.py:112
  165.8 163.1 %all-gather.42.cloned.1.call-start = ((), (), s32[]{:S(2)}) async-start(), calls=%async_computation.26 | async-start | bytes 1474560 | tf_op jit(solution)/shard_map/all_gather | solution.py:113
  166.4 211.9 %all-gather.24.cloned.1.call-start = ((), (), s32[]{:S(2)}) async-start(), calls=%async_computation.9 | async-start | bytes 4024320 | tf_op jit(solution)/shard_map/all_gather | solution.py:142
  332.9 91.9 %all-gather.26.cloned.1.call-start = ((), (), s32[]{:S(2)}) async-start(), calls=%async_computation.10 | async-start | bytes 4024320 | tf_op jit(solution)/shard_map/all_gather | solution.py:217
  367.0 187.8 %all-reduce.20.cloned.1.call-start = ((), (), s32[]{:S(2)}) async-start(), calls=%async_computation.29 | async-start | bytes 9732096
  439.1 209.6 %all-gather.28.cloned.1.call-start = ((), (), s32[]{:S(2)}) async-start(), calls=%async_computation.11 | async-start | bytes 4024320 | tf_op jit(solution)/shard_map/all_gather | solution.py:217
  603.5 135.1 %all-reduce.18.cloned.1.call-start = ((), (), s32[]{:S(2)}) async-start(), calls=%async_computation.28 | async-start | bytes 4866048
  663.0 201.1 %reduce-scatter.21.cloned.1.call-start = ((), (), s32[]{:S(2)}) async-start(), calls=%async_computation.13 | async-start | bytes 7299072 | tf_op jit(solution)/shard_map/reduce_scatter | solution.py:280
  668.5 321.3 %reduce-scatter.19.cloned.1.call-start = ((), (), s32[]{:S(2)}) async-start(), calls=%async_computation.12 | async-start | bytes 7299072 | tf_op jit(solution)/shard_map/reduce_scatter | solution.py:280
  756.2 279.5 %reduce-scatter.29.cloned.1.call-start = ((), (), s32[]{:S(2)}) async-start(), calls=%async_computation.18 | async-start | bytes 3981312 | tf_op jit(solution)/shard_map/reduce_scatter | solution.py:236
  764.1 316.3 %reduce-scatter.27.cloned.1.call-start = ((), (), s32[]{:S(2)}) async-start(), calls=%async_computation.17 | async-start | bytes 3981312 | tf_op jit(solution)/shard_map/reduce_scatter | solution.py:236
  771.7 353.1 %reduce-scatter.33.cloned.1.call-start = ((), (), s32[]{:S(2)}) async-start(), calls=%async_computation.21 | async-start | bytes 3981312 | tf_op jit(solution)/shard_map/reduce_scatter | solution.py:239
  779.5 390.0 %reduce-scatter.31.cloned.1.call-start = ((), (), s32[]{:S(2)}) async-start(), calls=%async_computation.20 | async-start | bytes 3981312 | tf_op jit(solution)/shard_map/reduce_scatter | solution.py:239
  787.7 484.5 %reduce-scatter.25.cloned.1.call-start = ((), (), s32[]{:S(2)}) async-start(), calls=%async_computation.16 | async-start | bytes 2433024 | tf_op jit(solution)/shard_map/reduce_scatter | solution.py:281
  790.7 585.7 %reduce-scatter.23.cloned.1.call-start = ((), (), s32[]{:S(2)}) async-start(), calls=%async_computation.15 | async-start | bytes 2433024 | tf_op jit(solution)/shard_map/reduce_scatter | solution.py:281
  792.7 612.4 %all-gather.30.cloned.1.call-start = ((), (), s32[]{:S(2)}) async-start(), calls=%async_computation.14 | async-start | bytes 1990656 | tf_op jit(solution)/shard_map/all_gather | solution.py:300
  865.1 306.7 %copy-start.24 = (bf16[197,768]{1,0:T(8,128)(2,1)S(1)}, bf16[197,768]{1,0:T(8,128)(2,1)}, u32[]{:S(2)}) copy-start(bf16[197,768]{1,0:T(8,128)(2,1)} %copy-done.23) | copy-start | bytes 907780
  865.1 306.7 %copy-start.69 = (f32[197,3]{0,1:T(4,128)S(1)}, f32[197,3]{0,1:T(4,128)}, u32[]{:S(2)}) copy-start(f32[197,3]{0,1:T(4,128)} %copy-done.68) | copy-start | bytes 7096
  991.5 486.4 %all-gather.32.cloned.1.call-start = ((), (), s32[]{:S(2)}) async-start(), calls=%async_computation.19 | async-start | bytes 7962624 | tf_op jit(solution)/shard_map/all_gather | solution.py:309
  1082.5 466.9 %all-gather.34.cloned.1.call-start = ((), (), s32[]{:S(2)}) async-start(), calls=%async_computation.22 | async-start | bytes 7962624 | tf_op jit(solution)/shard_map/all_gather | solution.py:312
  (116 other events, 3490.9 us)
Sparse Core Ops, SparseCore 0:
  10.5 51.3 all-gather.35
  64.3 27.7 all-gather.37
  96.2 44.5 all-gather.21
  165.4 83.6 all-reduce.15
  251.3 47.4 all-gather.39
  301.1 27.7 all-gather.41
  333.0 45.2 all-gather.23
  380.1 44.5 all-gather.25
  439.2 115.4 all-reduce.19
  603.6 45.0 all-gather.27
  663.1 75.4 all-reduce.17
  744.7 119.3 reduce-scatter.20
  871.3 118.4 reduce-scatter.18
  992.5 43.1 reduce-scatter.28
  1038.0 42.2 reduce-scatter.26
  1082.5 42.2 reduce-scatter.32
  1127.1 42.2 reduce-scatter.30
  1174.6 97.5 reduce-scatter.24
  1278.3 98.0 reduce-scatter.22
  1378.5 26.6 all-gather.29
  1407.3 70.5 all-gather.31
  1479.5 69.8 all-gather.33
where the time goes:
time: 1570 us
  waiting for transfers between devices  1050 us (67%)
  blocking collectives  168 us (11%)
  matrix products  122 us (8%)
  other arithmetic  104 us (7%)
  local copies, waits for them, and re-layouts  99.4 us (6%)
  between operations  18.2 us (1%)
    unnamed x25, waiting for transfers between devices  207 us
    reduce_scatter x2, waiting for transfers between devices, body(): lax.psum_scatter(block_terms[2], ('shard', 'replica'), scatter_dimension=...  196 us
    reduce_scatter x2, waiting for transfers between devices, body(): lax.psum_scatter(block_terms[3], ('shard', 'replica'), scatter_dimension=...  112 us
    reduce_scatter x2, waiting for transfers between devices, body(): lax.psum_scatter(grad_in.astype(jnp.bfloat16), 'replica', scatter_dimensi...  88.8 us
    reduce_scatter x2, waiting for transfers between devices, body(): lax.psum_scatter(grad_out.astype(jnp.bfloat16), 'replica', scatter_dimens...  86.9 us
    all_gather x1, waiting for transfers between devices, body(): lax.all_gather(collected[5].astype(jnp.bfloat16), 'replica', axis=2, tile...  69.3 us
    all_gather x2, waiting for transfers between devices, body(): group_grad = lax.all_gather(grad_returned, 'shard', axis=1, tiled=True)  67.2 us
    all_gather x1, waiting for transfers between devices, body(): lax.all_gather(collected[6].astype(jnp.bfloat16), 'replica', axis=2, tile...  61.3 us
  transfers between devices with their start and end apart: 22, of which 22 were waited for; matrix products, arithmetic and copies ran while one was open for 12% of the time, Pallas kernels for 0%

commit v1 on v0

v1 whole, which is shorter than its diff:
```python
import functools

import jax
import jax.numpy as jnp
from jax import lax
from jax.experimental import pallas as pl
from jax.experimental.pallas import tpu as pltpu
from jax.sharding import PartitionSpec as P

HEADS = 12
HEAD_DIM = 64
SEQ = 197
LANES = 128
MESH = pl.DeviceIdType.MESH

precise = lax.Precision.HIGHEST
VMEM = pl.BlockSpec(memory_space=pltpu.VMEM)


def round_up(value, step):
    return (value + step - 1) // step * step


def greet(devices):
    barrier = pltpu.get_barrier_semaphore()
    for device in devices:
        pl.semaphore_signal(barrier, inc=1, device_id=device, device_id_type=MESH)
    pl.semaphore_wait(barrier, len(devices))


def group_peers(n):
    me = lax.axis_index("shard")
    rep = lax.axis_index("replica")
    return me, [(lax.rem(me + k, n), rep) for k in range(1, n)]


def gather_kernel(n, x_ref, o_ref, send, recv):
    me, peers = group_peers(n)
    greet(peers)
    copies = []
    for k, peer in enumerate(peers):
        copy = pltpu.make_async_remote_copy(
            src_ref=x_ref,
            dst_ref=o_ref.at[me],
            send_sem=send.at[k],
            recv_sem=recv.at[k],
            device_id=peer,
            device_id_type=MESH,
        )
        copy.start()
        copies.append(copy)
    o_ref[me] = x_ref[...]
    for copy in copies:
        copy.wait()


def gather_rows(n, rows):
    return pl.pallas_call(
        functools.partial(gather_kernel, n),
        out_shape=jax.ShapeDtypeStruct((n,) + rows.shape, rows.dtype),
        in_specs=[VMEM],
        out_specs=VMEM,
        scratch_shapes=[pltpu.SemaphoreType.DMA((n - 1,)), pltpu.SemaphoreType.DMA((n - 1,))],
        compiler_params=pltpu.CompilerParams(collective_id=0, has_side_effects=True),
        name="gather_rows",
    )(rows)


def scatter_kernel(n, count, *refs):
    parts = refs[:count]
    outs = refs[count : 2 * count]
    lands = refs[2 * count : 3 * count]
    send, recv = refs[3 * count :]
    me, peers = group_peers(n)
    greet(peers)
    copies = []
    for k, peer in enumerate(peers):
        for i in range(count):
            copy = pltpu.make_async_remote_copy(
                src_ref=parts[i].at[peer[0]],
                dst_ref=lands[i].at[k],
                send_sem=send.at[i, k],
                recv_sem=recv.at[i, k],
                device_id=peer,
                device_id_type=MESH,
            )
            copy.start()
            copies.append(copy)
    for copy in copies:
        copy.wait()
    for i in range(count):
        total = parts[i][me].astype(jnp.float32)
        for k in range(n - 1):
            total = total + lands[i][k].astype(jnp.float32)
        outs[i][...] = total


def scatter_rows(n, parts, call_id):
    count = len(parts)
    return pl.pallas_call(
        functools.partial(scatter_kernel, n, count),
        out_shape=[jax.ShapeDtypeStruct(part.shape[1:], jnp.float32) for part in parts],
        in_specs=[VMEM] * count,
        out_specs=[VMEM] * count,
        scratch_shapes=[pltpu.VMEM((n - 1,) + part.shape[1:], part.dtype) for part in parts]
        + [pltpu.SemaphoreType.DMA((count, n - 1)), pltpu.SemaphoreType.DMA((count, n - 1))],
        compiler_params=pltpu.CompilerParams(collective_id=call_id, has_side_effects=True),
        name="scatter_rows",
    )(*parts)


def weights_kernel(n, halved, whole, *refs):
    count = halved + whole
    ins = refs[:count]
    outs = refs[count : 2 * count]
    send, recv, pass_send, pass_recv = refs[2 * count :]
    me, peers = group_peers(n)
    rep = lax.axis_index("replica")
    core = lax.rem(rep, 2)
    sibling = (me, rep + 1 - 2 * core)
    greet(peers + [sibling])
    copies = [[] for _ in range(count)]
    for i in list(range(halved, count)) + list(range(halved)):
        for k, peer in enumerate(peers):
            if i < halved:
                source, target = ins[i].at[core], outs[i].at[me, core]
            else:
                source, target = ins[i], outs[i].at[me]
            copy = pltpu.make_async_remote_copy(
                src_ref=source,
                dst_ref=target,
                send_sem=send.at[i, k],
                recv_sem=recv.at[i, k],
                device_id=peer,
                device_id_type=MESH,
            )
            copy.start()
            copies[i].append(copy)
    for i in range(count):
        outs[i][me] = ins[i][...]
    passed = []
    for i in range(halved):
        for k in range(n - 1):
            copies[i][k].wait_recv()
            owner = lax.rem(me + n - 1 - k, n)
            copy = pltpu.make_async_remote_copy(
                src_ref=outs[i].at[owner, core],
                dst_ref=outs[i].at[owner, core],
                send_sem=pass_send.at[i, k],
                recv_sem=pass_recv.at[i, k],
                device_id=sibling,
                device_id_type=MESH,
            )
            copy.start()
            passed.append(copy)
    for i in range(halved, count):
        for copy in copies[i]:
            copy.wait_recv()
    for i in range(count):
        for copy in copies[i]:
            copy.wait_send()
    for copy in passed:
        copy.wait()


def gather_weights(n, halved, whole):
    arrays = [a.reshape(2, a.shape[0] // 2, a.shape[1]) for a in halved] + list(whole)
    count = len(arrays)
    outs = pl.pallas_call(
        functools.partial(weights_kernel, n, len(halved), len(whole)),
        out_shape=[jax.ShapeDtypeStruct((n,) + a.shape, a.dtype) for a in arrays],
        in_specs=[VMEM] * count,
        out_specs=[VMEM] * count,
        scratch_shapes=[
            pltpu.SemaphoreType.DMA((count, n - 1)),
            pltpu.SemaphoreType.DMA((count, n - 1)),
            pltpu.SemaphoreType.DMA((len(halved), n - 1)),
            pltpu.SemaphoreType.DMA((len(halved), n - 1)),
        ],
        compiler_params=pltpu.CompilerParams(collective_id=3, has_side_effects=True),
        name="gather_weights",
    )(*arrays)
    full = [o.reshape(n * a.shape[0], a.shape[1]) for o, a in zip(outs, halved)]
    return full, outs[len(halved) :]


def norm_forward(values, gain, bias):
    centre = values - jnp.mean(values, axis=-1, keepdims=True)
    spread = jnp.mean(centre * centre, axis=-1, keepdims=True)
    scaled = lax.rsqrt(spread + 1e-06)
    normal = centre * scaled
    return (normal * gain + bias, normal, scaled)


def norm_backward(upstream, gain, normal, scaled):
    inner = upstream * gain
    centred = inner - jnp.mean(inner, axis=-1, keepdims=True)
    result = scaled * (centred - normal * jnp.mean(inner * normal, axis=-1, keepdims=True))
    return (result, jnp.sum(upstream * normal, axis=0), jnp.sum(upstream, axis=0))


def gelu_slope(values):
    return (
        0.5 * (1.0 + lax.erf(values * 0.7071067811865476))
        + values * jnp.exp(-0.5 * values * values) * 0.3989422804014327
    )


def split_heads(packed):
    blocks = packed.reshape(packed.shape[0], 3, HEADS, HEAD_DIM)
    return (blocks[:, 0], blocks[:, 1], blocks[:, 2])


def head_scores(queries, key_rows):
    scores = jnp.einsum("qhd,khd->hqk", queries, key_rows, preferred_element_type=jnp.float32)
    seen = jnp.arange(key_rows.shape[0], dtype=jnp.int32) < SEQ
    return jnp.where(seen[None, None, :], scores * 0.125, -1e30)


def attend(packed):
    queries, key_rows, val_rows = split_heads(packed)
    scores = head_scores(queries, key_rows)
    log_total = jax.nn.logsumexp(scores, axis=-1, keepdims=True)
    weights = jnp.exp(scores - log_total).astype(jnp.bfloat16)
    result = jnp.einsum("hqk,khd->qhd", weights, val_rows, preferred_element_type=jnp.float32)
    return (result.astype(jnp.bfloat16).reshape(packed.shape[0], HEADS * HEAD_DIM), log_total)


def attend_back(packed, log_total, upstream):
    queries, key_rows, val_rows = split_heads(packed)
    weights = jnp.exp(head_scores(queries, key_rows) - log_total)
    incoming = upstream.reshape(queries.shape)
    grad_values = jnp.einsum(
        "hqk,qhd->khd", weights.astype(jnp.bfloat16), incoming, preferred_element_type=jnp.float32
    )
    grad_weights = jnp.einsum(
        "qhd,khd->hqk", incoming, val_rows, preferred_element_type=jnp.float32
    )
    inner = jnp.sum(weights * grad_weights, axis=-1, keepdims=True)
    grad_scores = (weights * (grad_weights - inner)).astype(jnp.bfloat16)
    grad_queries = (
        jnp.einsum("hqk,khd->qhd", grad_scores, key_rows, preferred_element_type=jnp.float32)
        * 0.125
    )
    grad_keys = (
        jnp.einsum("hqk,qhd->khd", grad_scores, queries, preferred_element_type=jnp.float32)
        * 0.125
    )
    stacked = jnp.stack([grad_queries, grad_keys, grad_values], axis=1)
    return stacked.astype(jnp.bfloat16).reshape(packed.shape)


def body(
    n,
    tokens,
    ln_gain,
    ln_bias,
    w_qkv,
    w_proj,
    w_router,
    expert_in,
    expert_out,
    image_count,
    expert_ids,
    slot_index,
    cotangent,
):
    count, width = tokens.shape
    rows = round_up(count, 16)
    layers, share = w_qkv.shape[:2]
    experts, units = expert_in.shape[1:3]
    slots = experts * units
    padded = ((0, rows - count), (0, 0))
    live = (jnp.arange(rows, dtype=jnp.int32) // SEQ < image_count[0]).astype(jnp.float32)[:, None]
    kinds = jnp.arange(experts, dtype=jnp.int32)
    hits = (expert_ids[..., None] == kinds) & (slot_index[..., None] >= 0)
    own_mask = jnp.sum(hits.astype(jnp.float32), axis=2)
    own_mask = jnp.pad(own_mask, ((0, 0),) + padded)
    mask_block = jnp.swapaxes(own_mask, 0, 1).reshape(rows, layers * experts)
    mask_block = jnp.pad(mask_block, ((0, 0), (0, LANES - layers * experts)))
    smalls = jnp.concatenate(
        [
            ln_gain.reshape(2 * layers, share),
            ln_bias.reshape(2 * layers, share),
            jnp.swapaxes(w_router, 1, 2).reshape(layers * experts, share),
        ]
    )
    small_rows = smalls.shape[0]
    smalls = jnp.pad(
        smalls,
        ((0, round_up(small_rows, 16) - small_rows), (0, round_up(share, LANES) - share)),
    )
    (qkv_first, proj_first), (small_all, mask_all) = gather_weights(
        n, (w_qkv[0], w_proj[0]), (smalls, mask_block.astype(jnp.bfloat16))
    )
    small_all = jnp.swapaxes(small_all[:, :small_rows, :share], 0, 1).reshape(small_rows, width)
    gains = small_all[: 2 * layers].astype(jnp.float32).reshape(layers, 2, width)
    biases = small_all[2 * layers : 4 * layers].astype(jnp.float32).reshape(layers, 2, width)
    routers = small_all[4 * layers :].reshape(layers, experts, width)
    masks = mask_all.reshape(n * rows, LANES)[:, : layers * experts].astype(jnp.float32)
    masks = masks.reshape(n * rows, layers, experts)
    qkv_all = [qkv_first]
    proj_all = [proj_first]
    for layer_idx in range(1, layers):
        qkv_all.append(lax.all_gather(w_qkv[layer_idx], "shard", axis=0, tiled=True))
        proj_all.append(lax.all_gather(w_proj[layer_idx], "shard", axis=0, tiled=True))
    state = jnp.pad(tokens.astype(jnp.float32), padded)
    saved = []
    for layer_idx in range(layers):
        gain = gains[layer_idx]
        bias = biases[layer_idx]
        first_out, first_normal, first_scaled = norm_forward(state, gain[0], bias[0])
        first_low = first_out.astype(jnp.bfloat16)
        packed = jnp.dot(first_low, qkv_all[layer_idx], preferred_element_type=jnp.float32).astype(
            jnp.bfloat16
        )
        attended, log_total = attend(packed)
        after = state + jnp.dot(attended, proj_all[layer_idx], preferred_element_type=jnp.float32)
        second_out, second_normal, second_scaled = norm_forward(after, gain[1], bias[1])
        second_low = second_out.astype(jnp.bfloat16)
        group_rows = gather_rows(n, second_low).reshape(n * rows, width)
        logits = lax.dot_general(
            group_rows,
            routers[layer_idx],
            (((1,), (1,)), ((), ())),
            preferred_element_type=jnp.float32,
        )
        group_probs = jax.nn.softmax(logits, axis=-1)
        gates = group_probs * masks[:, layer_idx]
        wide_gates = jnp.repeat(gates, units, axis=1, total_repeat_length=slots)
        table_in = expert_in[layer_idx].reshape(slots, width)
        table_out = expert_out[layer_idx].reshape(slots, width)
        before = lax.dot_general(
            group_rows, table_in, (((1,), (1,)), ((), ())), preferred_element_type=jnp.float32
        )
        raw_hidden = jax.nn.gelu(before, approximate=False)
        hidden = raw_hidden.astype(jnp.bfloat16)
        scaled_hidden = (raw_hidden * wide_gates).astype(jnp.bfloat16)
        partial_rows = jnp.dot(scaled_hidden, table_out, preferred_element_type=jnp.float32)
        (combined,) = scatter_rows(
            n, [partial_rows.astype(jnp.bfloat16).reshape(n, rows, width)], 1
        )
        me = lax.axis_index("shard")
        probs = lax.dynamic_slice_in_dim(group_probs, me * rows, rows, axis=0)
        saved.append(
            (
                first_normal,
                first_scaled,
                first_low,
                packed,
                attended,
                log_total,
                second_normal,
                second_scaled,
                second_low,
                probs,
                wide_gates,
                group_rows,
                before,
                hidden,
                scaled_hidden,
                table_in,
                table_out,
            )
        )
        state = after + combined
    mixed = (state * live).astype(jnp.bfloat16)
    grad_state = jnp.pad(cotangent.astype(jnp.float32), padded) * live
    dense_lists = [None] * layers
    expert_lists = [None] * layers
    for layer_idx in reversed(range(layers)):
        (
            first_normal,
            first_scaled,
            first_low,
            packed,
            attended,
            log_total,
            second_normal,
            second_scaled,
            second_low,
            probs,
            wide_gates,
            group_rows,
            before,
            hidden,
            scaled_hidden,
            table_in,
            table_out,
        ) = saved[layer_idx]
        gain = gains[layer_idx]
        group_grad = gather_rows(n, grad_state.astype(jnp.bfloat16)).reshape(n * rows, width)
        ungated = lax.dot_general(
            group_grad, table_out, (((1,), (1,)), ((), ())), preferred_element_type=jnp.float32
        )
        gate_terms = jnp.sum(
            (ungated * hidden.astype(jnp.float32)).reshape(n, rows, experts, units), axis=-1
        )
        gate_terms = jnp.pad(
            jnp.swapaxes(gate_terms, 1, 2),
            ((0, 0), (0, round_up(experts, 8) - experts), (0, round_up(rows, LANES) - rows)),
        )
        grad_before = (ungated * wide_gates * gelu_slope(before)).astype(jnp.bfloat16)
        row_terms = jnp.dot(grad_before, table_in, preferred_element_type=jnp.float32)
        grad_rows, grad_gates = scatter_rows(
            n, [row_terms.astype(jnp.bfloat16).reshape(n, rows, width), gate_terms], 2
        )
        grad_out = lax.dot_general(
            scaled_hidden, group_grad, (((0,), (0,)), ((), ())), preferred_element_type=jnp.float32
        )
        grad_in = lax.dot_general(
            grad_before, group_rows, (((0,), (0,)), ((), ())), preferred_element_type=jnp.float32
        )
        expert_lists[layer_idx] = [
            lax.psum_scatter(term.astype(jnp.bfloat16), "replica", scatter_dimension=0, tiled=True)
            for term in (grad_in, grad_out)
        ]
        grad_probs = grad_gates[:experts, :rows].T * own_mask[layer_idx]
        grad_logits = probs * (grad_probs - jnp.sum(probs * grad_probs, axis=-1, keepdims=True))
        router_wide = routers[layer_idx].astype(jnp.float32)
        grad_router = jnp.dot(second_low.astype(jnp.float32).T, grad_logits, precision=precise)
        grad_second = grad_rows + jnp.dot(grad_logits, router_wide, precision=precise)
        norm_part, gain_second, bias_second = norm_backward(
            grad_second, gain[1], second_normal, second_scaled
        )
        grad_after = grad_state + norm_part
        grad_proj_in = grad_after.astype(jnp.bfloat16)
        grad_proj = jnp.dot(attended.T, grad_proj_in, preferred_element_type=jnp.float32)
        grad_attended = jnp.dot(
            grad_proj_in, proj_all[layer_idx].T, preferred_element_type=jnp.float32
        ).astype(jnp.bfloat16)
        grad_packed = attend_back(packed, log_total, grad_attended)
        grad_qkv = jnp.dot(first_low.T, grad_packed, preferred_element_type=jnp.float32)
        grad_first = jnp.dot(grad_packed, qkv_all[layer_idx].T, preferred_element_type=jnp.float32)
        norm_first, gain_first, bias_first = norm_backward(
            grad_first, gain[0], first_normal, first_scaled
        )
        grad_state = grad_after + norm_first
        vectors = jnp.stack([gain_first, gain_second, bias_first, bias_second], axis=1)
        edge = jnp.concatenate([grad_router, vectors], axis=1)
        edge = jnp.pad(edge, ((0, 0), (0, LANES - edge.shape[1])))
        dense = jnp.concatenate(
            [
                grad_qkv.astype(jnp.bfloat16),
                grad_proj.astype(jnp.bfloat16),
                edge.astype(jnp.bfloat16),
            ],
            axis=1,
        )
        dense = lax.psum_scatter(dense, "shard", scatter_dimension=0, tiled=True)
        dense_lists[layer_idx] = lax.psum(dense, "replica").astype(jnp.float32)
    expert_grads = []
    for which in range(2):
        expert_grads.append(
            jnp.stack(
                [
                    lax.all_gather(item[which], "replica", axis=0, tiled=True)
                    .astype(jnp.float32)
                    .reshape(experts, units, width)
                    for item in expert_lists
                ]
            )
        )
    dense = jnp.stack(dense_lists)
    packed_width = w_qkv.shape[2]
    start = packed_width + width
    edges = dense[:, :, start : start + experts + 4]
    vectors = jnp.swapaxes(edges[:, :, experts:], 1, 2)
    return (
        mixed[:count],
        grad_state[:count],
        vectors[:, 0:2],
        vectors[:, 2],
        vectors[:, 3],
        dense[:, :, :packed_width],
        dense[:, :, packed_width:start],
        edges[:, :, :experts],
        expert_grads[0],
        expert_grads[1],
    )


def solution(mesh):
    placed = (
        P(("shard", "replica"), None),
        P(None, None, "shard"),
        P(None, None, "shard"),
        P(None, "shard", None),
        P(None, "shard", None),
        P(None, "shard", None),
        P(None, None, "shard", None),
        P(None, None, "shard", None),
        P(("shard", "replica")),
        P(None, ("shard", "replica"), None),
        P(None, ("shard", "replica"), None),
        P(("shard", "replica"), None),
    )
    return jax.shard_map(
        functools.partial(body, mesh.shape["shard"]),
        mesh=mesh,
        in_specs=placed,
        out_specs=(
            P(("shard", "replica"), None),
            P(("shard", "replica"), None),
            P(None, None, "shard"),
            P(None, "shard"),
            P(None, "shard"),
            P(None, "shard", None),
            P(None, "shard", None),
            P(None, "shard", None),
            P(None, None, "shard", None),
            P(None, None, "shard", None),
        ),
        check_vma=False,
    )
```

time: 1570 us -> 964 us (0.61)
  waiting for transfers between devices: 1050 us -> 393 us
  Pallas kernels: 0 us -> 204 us
  blocking collectives: 168 us -> 0 us
  matrix products: 122 us -> 171 us
  other arithmetic: 104 us -> 66 us
    reduce_scatter x8 -> x6, waiting for transfers between devices: 484 us -> 199 us  [the longest x4 180 us: body(): lax.psum_scatter(term.astype(jnp.bfloat16), 'replica', scatter_dimension=...]
    unnamed x25 -> x13, waiting for transfers between devices: 207 us -> 0.21 us
    pallas_call x0 -> x9, Pallas kernels: none -> 204 us  [the longest x4 88.2 us: gather_rows(): pl.pallas_call(functools.partial(gather_kernel, n), out_shape=jax.ShapeDt...]
    all_gather x10 -> x0, blocking collectives: 127 us -> none  [the longest x2 24.7 us: body(): lax.all_gather(w_router[layer_idx], 'shard', axis=0, tiled=True)]
    all_gather x7 -> x4, waiting for transfers between devices: 264 us -> 153 us  [body(): lax.all_gather(item[which], 'replica', axis=0, tiled=True)]
    all_gather x2 -> x1, waiting for transfers between devices: 53.1 us -> 0.01 us  [body(): lax.all_gather(w_qkv[layer_idx], 'shard', axis=0, tiled=True)]
    dot_general x38 -> x36, matrix products: 109 us -> 161 us  [the longest x2 40.9 us: body(): lax.dot_general(group_grad, table_out, (((1,), (1,)), ((), ())), preferre...]
    all_gather x2 -> x1, waiting for transfers between devices: 44.8 us -> 0.01 us  [body(): lax.all_gather(w_proj[layer_idx], 'shard', axis=0, tiled=True)]
  transfers between devices with their start and end apart: 22 -> 13, of which waited for: 22 -> 10; matrix products, arithmetic and copies ran while one was open for 12% -> 22% of each run, Pallas kernels for 0% -> 18%
where the time goes in v1:
time: 964 us; the launch traced here: 953 us
  waiting for transfers between devices  393 us (41%)
  Pallas kernels  204 us (21%)
  matrix products  171 us (18%)
  local copies, waits for them, and re-layouts  103 us (11%)
  other arithmetic  66 us (7%)
  between operations  16.3 us (2%)
    reduce_scatter x4, waiting for transfers between devices, body(): lax.psum_scatter(term.astype(jnp.bfloat16), 'replica', scatter_dimension=...  180 us
    all_gather x4, waiting for transfers between devices, body(): lax.all_gather(item[which], 'replica', axis=0, tiled=True)  153 us
    pallas_call x4, Pallas kernels, gather_rows(): pl.pallas_call(functools.partial(gather_kernel, n), out_shape=jax.ShapeDt...  88.2 us
    pallas_call x4, Pallas kernels, scatter_rows(): pl.pallas_call(functools.partial(scatter_kernel, n, count), out_shape=[ja...  68.9 us
    pallas_call x1, Pallas kernels, gather_weights(): pl.pallas_call(functools.partial(weights_kernel, n, len(halved), len(whol...  47.3 us
    dot_general x2, matrix products, body(): lax.dot_general(group_grad, table_out, (((1,), (1,)), ((), ())), preferre...  40.9 us
    psum x1, waiting for transfers between devices, body(): dense_lists[layer_idx] = lax.psum(dense, 'replica').astype(jnp.float32)  40.6 us
    gather x4, local copies, waits for them, and re-layouts, body(): wide_gates = jnp.repeat(gates, units, axis=1, total_repeat_length=slots)  32.9 us
  transfers between devices with their start and end apart: 13, of which 10 were waited for; matrix products, arithmetic and copies ran while one was open for 22% of the time, Pallas kernels for 18%

profile of v1, /device:TPU:0, one launch (start us, length us, event | category | flops | bytes accessed | tf_op | source)
XLA Modules:
  0.0 953.5 jit_solution(11345096849400476667)
XLA Ops:
  13.4 47.3 %gather_weights.1 = (bf16[4,2,96,2304]{3,2,1,0:T(8,128)(2,1)}, bf16[4,2,96,768]{3,2,1,0:T(8,128)(2,1)}, bf16[4,16,256]{2,1,0:T(8,128)(2,1)}, bf16[4,208,128]{2,1,0:T(8,128)(2,1)}) custom-call(bf16[2,96,2304]{2,1,0:T(8,128)(2,1)} %bitcast.286, bf16[2,96,768]{2,1,0:T(8,128)(2,1)} %bitcast.310, bf16[16,256]{1,0:T(8,128)(2,1)} %fusion.83.refs_2_, ...), custom_call_target="tpu_custom_call" | custom-call | tf_op jit(solution)/shard_map/gather_weights/pallas_call | solution.py:169
  72.7 21.9 %gather_rows.4 = bf16[4,208,768]{2,1,0:T(8,128)(2,1)} custom-call(bf16[208,768]{1,0:T(8,128)(2,1)} %add_convert_fusion.2.x_ref), custom_call_target="tpu_custom_call" | custom-call | tf_op jit(solution)/shard_map/gather_rows/pallas_call | solution.py:58
  125.0 23.1 %fusion.19 = (bf16[832,2304]{1,0:T(8,128)(2,1)S(1)}, bf16[832,2304]{1,0:T(8,128)(2,1)}, f32[832,2304]{1,0:T(8,128)}) fusion(f32[2304,832]{0,1:T(8,128)} %copy.127, bf16[832,768]{1,0:T(8,128)(2,1)S(1)} %bitcast.267, bf16[2304,768]{1,0:T(8,128)(2,1)} %bitcast.280), kind=kOutput, calls=%fused_computation.30 | convolution fusion | flops 3072835584 | bytes 27820032 | tf_op jit(solution)/shard_map/dot_general | solution.py:333
  152.4 19.5 %scatter_rows.4 = f32[208,768]{1,0:T(8,128)} custom-call(bf16[4,208,768]{2,1,0:T(8,128)(2,1)} %bitcast.307), custom_call_target="tpu_custom_call" | custom-call | tf_op jit(solution)/shard_map/scatter_rows/pallas_call | solution.py:100
  174.2 18.4 %gather_rows.6 = bf16[4,208,768]{2,1,0:T(8,128)(2,1)} custom-call(bf16[208,768]{1,0:T(8,128)(2,1)} %fusion.55.x_ref), custom_call_target="tpu_custom_call" | custom-call | tf_op jit(solution)/shard_map/gather_rows/pallas_call | solution.py:58
  206.1 18.4 %gather_rows.5 = bf16[4,208,768]{2,1,0:T(8,128)(2,1)} custom-call(bf16[208,768]{1,0:T(8,128)(2,1)} %add_convert_fusion.x_ref), custom_call_target="tpu_custom_call" | custom-call | tf_op jit(solution)/shard_map/gather_rows/pallas_call | solution.py:58
  252.1 27.3 %convert_multiply_fusion.1 = (f32[832,2304]{1,0:T(8,128)}, f32[832,2304]{1,0:T(8,128)}, bf16[832,2304]{1,0:T(8,128)(2,1)S(1)}) fusion(f32[832,2304]{1,0:T(8,128)} %fusion.116, f32[2304,832]{0,1:T(8,128)} %copy.131, bf16[832,768]{1,0:T(8,128)(2,1)} %bitcast.300, bf16[2304,768]{1,0:T(8,128)(2,1)} %bitcast.278), kind=kOutput, calls=%fused_computation.32 | convolution fusion | flops 3093921792 | bytes 39321600 | tf_op jit(solution)/shard_map/dot_general | solution.py:393
  283.6 12.8 %reshape.397 = f32[4,208,3,768]{3,2,1,0:T(4,128)} reshape(f32[832,2304]{1,0:T(8,128)} %get-tuple-element.118) | data formatting | bytes 15335424 | tf_op jit(solution)/shard_map/reshape | solution.py:397
  304.4 18.1 %scatter_rows.6 = (f32[208,768]{1,0:T(8,128)}, f32[8,256]{1,0:T(8,128)}) custom-call(bf16[4,208,768]{2,1,0:T(8,128)(2,1)} %bitcast.304, f32[4,8,256]{2,1,0:T(8,128)} %pad.53.refs_1_), custom_call_target="tpu_custom_call" | custom-call | tf_op jit(solution)/shard_map/scatter_rows/pallas_call | solution.py:100
  350.2 29.5 %gather_rows.7 = bf16[4,208,768]{2,1,0:T(8,128)(2,1)} custom-call(bf16[208,768]{1,0:T(8,128)(2,1)} %get-tuple-element.116.x_ref), custom_call_target="tpu_custom_call" | custom-call | tf_op jit(solution)/shard_map/gather_rows/pallas_call | solution.py:58
  379.7 13.7 %convert_multiply_fusion = (f32[832,2304]{1,0:T(8,128)}, bf16[832,2304]{1,0:T(8,128)(2,1)}) fusion(bf16[832,2304]{1,0:T(8,128)(2,1)} %get-tuple-element.125, f32[832,2304]{1,0:T(8,128)} %get-tuple-element.153, f32[2304,832]{0,1:T(8,128)} %copy.127, bf16[832,768]{1,0:T(8,128)(2,1)} %bitcast.302, bf16[2304,768]{1,0:T(8,128)(2,1)} %bitcast.282), kind=kOutput, calls=%fused_computation.31 | convolution fusion | flops 2969321472 | bytes 35487744 | tf_op jit(solution)/shard_map/dot_general | solution.py:393
  393.4 12.9 %reshape.398 = f32[4,208,3,768]{3,2,1,0:T(4,128)} reshape(f32[832,2304]{1,0:T(8,128)} %get-tuple-element.129) | data formatting | bytes 15335424 | tf_op jit(solution)/shard_map/reshape | solution.py:397
  420.1 13.9 %scatter_rows.7 = (f32[208,768]{1,0:T(8,128)}, f32[8,256]{1,0:T(8,128)}) custom-call(bf16[4,208,768]{2,1,0:T(8,128)(2,1)} %bitcast.305, f32[4,8,256]{2,1,0:T(8,128)} %pad.54.refs_1_), custom_call_target="tpu_custom_call" | custom-call | tf_op jit(solution)/shard_map/scatter_rows/pallas_call | solution.py:100
  500.3 18.8 %reduce-scatter.7.cloned.1.call-done = bf16[192,3200]{1,0:T(8,128)(2,1)} async-done(((bf16[768,3200]{1,0:T(8,128)(2,1)}), bf16[192,3200]{1,0:T(8,128)(2,1)}) %reduce-scatter.7.cloned.1.call-update) | async-done | bytes 1228816 | tf_op jit(solution)/shard_map/reduce_scatter | solution.py:450
  519.2 46.5 %reduce-scatter.13.cloned.1.call-done = bf16[288,768]{1,0:T(8,128)(2,1)} async-done(((bf16[2304,768]{1,0:T(8,128)(2,1)}), bf16[288,768]{1,0:T(8,128)(2,1)}) %reduce-scatter.13.cloned.1.call-update) | async-done | bytes 442384 | tf_op jit(solution)/shard_map/reduce_scatter | solution.py:415
  565.8 44.6 %reduce-scatter.11.cloned.1.call-done = bf16[288,768]{1,0:T(8,128)(2,1)} async-done(((bf16[2304,768]{1,0:T(8,128)(2,1)}), bf16[288,768]{1,0:T(8,128)(2,1)}) %reduce-scatter.11.cloned.1.call-update) | async-done | bytes 442384 | tf_op jit(solution)/shard_map/reduce_scatter | solution.py:415
  610.4 44.6 %reduce-scatter.17.cloned.1.call-done = bf16[288,768]{1,0:T(8,128)(2,1)} async-done(((bf16[2304,768]{1,0:T(8,128)(2,1)}), bf16[288,768]{1,0:T(8,128)(2,1)}) %reduce-scatter.17.cloned.1.call-update) | async-done | bytes 442384 | tf_op jit(solution)/shard_map/reduce_scatter | solution.py:415
  655.3 44.6 %reduce-scatter.15.cloned.1.call-done = bf16[288,768]{1,0:T(8,128)(2,1)} async-done(((bf16[2304,768]{1,0:T(8,128)(2,1)}), bf16[288,768]{1,0:T(8,128)(2,1)}) %reduce-scatter.15.cloned.1.call-update) | async-done | bytes 442384 | tf_op jit(solution)/shard_map/reduce_scatter | solution.py:415
  707.3 17.3 %scatter_rows.5 = f32[208,768]{1,0:T(8,128)} custom-call(bf16[4,208,768]{2,1,0:T(8,128)(2,1)} %bitcast.306), custom_call_target="tpu_custom_call" | custom-call | tf_op jit(solution)/shard_map/scatter_rows/pallas_call | solution.py:100
  727.6 40.6 %all-reduce.12.cloned.1.call-done = (bf16[1,192,3200]{2,1,0:T(8,128)(2,1)}, bf16[1,192,3200]{2,1,0:T(8,128)(2,1)}) async-done(((bf16[1,192,3200]{2,1,0:T(8,128)(2,1)}, bf16[1,192,3200]{2,1,0:T(8,128)(2,1)}), (bf16[1,192,3200]{2,1,0:T(8,128)(2,1)}, bf16[1,192,3200]{2,1,0:T(8,128)(2,1)})) %all-reduce.12.cloned.1.call-update) | async-done | bytes 2457616 | tf_op jit(solution)/shard_map/psum | solution.py:451
  775.2 36.0 %all-gather.11.cloned.1.call-done = bf16[2304,768]{1,0:T(8,128)(2,1)} async-done(((bf16[288,768]{1,0:T(8,128)(2,1)}), bf16[2304,768]{1,0:T(8,128)(2,1)}) %all-gather.11.cloned.1.call-update) | async-done | bytes 3538960 | tf_op jit(solution)/shard_map/all_gather | solution.py:457
  811.1 42.2 %all-gather.9.cloned.1.call-done = bf16[2304,768]{1,0:T(8,128)(2,1)} async-done(((bf16[288,768]{1,0:T(8,128)(2,1)}), bf16[2304,768]{1,0:T(8,128)(2,1)}) %all-gather.9.cloned.1.call-update) | async-done | bytes 3538960 | tf_op jit(solution)/shard_map/all_gather | solution.py:457
  862.6 32.7 %all-gather.15.cloned.1.call-done = bf16[2304,768]{1,0:T(8,128)(2,1)} async-done(((bf16[288,768]{1,0:T(8,128)(2,1)}), bf16[2304,768]{1,0:T(8,128)(2,1)}) %all-gather.15.cloned.1.call-update) | async-done | bytes 3538960 | tf_op jit(solution)/shard_map/all_gather | solution.py:457
  895.3 42.2 %all-gather.13.cloned.1.call-done = bf16[2304,768]{1,0:T(8,128)(2,1)} async-done(((bf16[288,768]{1,0:T(8,128)(2,1)}), bf16[2304,768]{1,0:T(8,128)(2,1)}) %all-gather.13.cloned.1.call-update) | async-done | bytes 3538960 | tf_op jit(solution)/shard_map/all_gather | solution.py:457
  (375 shorter events, 250.3 us)
Async XLA Ops:
  7.2 55.4 %copy-start.74 = (s32[2304]{0:T(1024)S(1)}, s32[2304]{0:T(1024)}, u32[]{:S(2)}) copy-start(s32[2304]{0:T(1024)} %constant.238) | copy-start | bytes 27652
  7.3 54.9 %copy-start.18 = (bf16[197,768]{1,0:T(8,128)(2,1)S(1)}, bf16[197,768]{1,0:T(8,128)(2,1)}, u32[]{:S(2)}) copy-start(bf16[197,768]{1,0:T(8,128)(2,1)} %param.18) | copy-start | bytes 907780
  7.3 185.8 %all-gather.17.cloned.1.call-start = ((), (), s32[]{:S(2)}) async-start(), calls=%async_computation.16 | async-start | bytes 4423680 | tf_op jit(solution)/shard_map/all_gather | solution.py:305
  10.2 192.2 %all-gather.19.cloned.1.call-start = ((), (), s32[]{:S(2)}) async-start(), calls=%async_computation.17 | async-start | bytes 1474560 | tf_op jit(solution)/shard_map/all_gather | solution.py:306
  11.1 489.2 %reduce-scatter.9.cloned.1.call-start = ((), (), s32[]{:S(2)}) async-start(), calls=%async_computation.7 | async-start | bytes 6144000 | tf_op jit(solution)/shard_map/reduce_scatter | solution.py:450
  11.2 188.7 %copy-start.57 = (pred[208]{0:T(512)(128)(4,1)}, pred[208]{0:T(512)(128)(4,1)S(1)}, u32[]{:S(2)}) copy-start(pred[208]{0:T(512)(128)(4,1)S(1)} %iota_compare_fusion.3) | copy-start | bytes 628
  62.2 111.0 %copy-start.79 = (f32[208]{0:T(256)}, f32[208]{0:T(256)S(1)}, u32[]{:S(2)}) copy-start(f32[208]{0:T(256)S(1)} %compare_convert_fusion) | copy-start | bytes 2500
  64.2 43.3 %copy-start.52 = (bf16[3,768]{1,0:T(4,128)(2,1)}, bf16[3,768]{1,0:T(4,128)(2,1)S(1)}, u32[]{:S(2)}) copy-start(bf16[3,768]{1,0:T(4,128)(2,1)S(1)} %squeeze.68) | copy-start | bytes 13828
  71.5 100.4 %copy-start.2 = (f32[208,768]{1,0:T(8,128)}, f32[208,768]{1,0:T(8,128)S(1)}, u32[]{:S(2)}) copy-start(f32[208,768]{1,0:T(8,128)S(1)} %get-tuple-element.150) | copy-start | bytes 1916932
  71.5 29.6 %copy-start.60 = (f32[208]{0:T(256)}, f32[208]{0:T(256)S(1)}, u32[]{:S(2)}) copy-start(f32[208]{0:T(256)S(1)} %broadcast_multiply_fusion.11) | copy-start | bytes 2500
  71.7 29.3 %copy-start.66 = (f32[208]{0:T(256)}, f32[208]{0:T(256)S(1)}, u32[]{:S(2)}) copy-start(f32[208]{0:T(256)S(1)} %add_rsqrt_fusion.2) | copy-start | bytes 2500
  192.7 31.8 %copy-start.54 = (bf16[3,768]{1,0:T(4,128)(2,1)}, bf16[3,768]{1,0:T(4,128)(2,1)S(1)}, u32[]{:S(2)}) copy-start(bf16[3,768]{1,0:T(4,128)(2,1)S(1)} %squeeze.75) | copy-start | bytes 13828
  205.2 30.5 %copy-start.73 = (f32[208]{0:T(256)}, f32[208]{0:T(256)S(1)}, u32[]{:S(2)}) copy-start(f32[208]{0:T(256)S(1)} %add_rsqrt_fusion) | copy-start | bytes 2500
  252.1 27.3 %copy-start.26 = (bf16[1,3,768,768]{3,2,1,0:T(8,128)(2,1)S(1)}, bf16[1,3,768,768]{3,2,1,0:T(8,128)(2,1)}, u32[]{:S(2)}) copy-start(bf16[1,3,768,768]{3,2,1,0:T(8,128)(2,1)} %get-tuple-element.131) | copy-start | bytes 10616836
  347.7 171.4 %reduce-scatter.7.cloned.1.call-start = ((), (), s32[]{:S(2)}) async-start(), calls=%async_computation.6 | async-start | bytes 6144000 | tf_op jit(solution)/shard_map/reduce_scatter | solution.py:450
  459.6 106.1 %reduce-scatter.13.cloned.1.call-start = ((), (), s32[]{:S(2)}) async-start(), calls=%async_computation.10 | async-start | bytes 3981312 | tf_op jit(solution)/shard_map/reduce_scatter | solution.py:415
  468.4 142.0 %reduce-scatter.11.cloned.1.call-start = ((), (), s32[]{:S(2)}) async-start(), calls=%async_computation.8 | async-start | bytes 3981312 | tf_op jit(solution)/shard_map/reduce_scatter | solution.py:415
  477.3 177.8 %reduce-scatter.17.cloned.1.call-start = ((), (), s32[]{:S(2)}) async-start(), calls=%async_computation.14 | async-start | bytes 3981312 | tf_op jit(solution)/shard_map/reduce_scatter | solution.py:415
  491.2 208.7 %reduce-scatter.15.cloned.1.call-start = ((), (), s32[]{:S(2)}) async-start(), calls=%async_computation.12 | async-start | bytes 3981312 | tf_op jit(solution)/shard_map/reduce_scatter | solution.py:415
  500.2 268.0 %all-reduce.12.cloned.1.call-start = ((), (), s32[]{:S(2)}) async-start(), calls=%async_computation.18 | async-start | bytes 4915200 | tf_op jit(solution)/shard_map/psum | solution.py:451
  519.2 292.0 %all-gather.11.cloned.1.call-start = ((), (), s32[]{:S(2)}) async-start(), calls=%async_computation.11 | async-start | bytes 3981312 | tf_op jit(solution)/shard_map/all_gather | solution.py:457
  565.7 287.6 %all-gather.9.cloned.1.call-start = ((), (), s32[]{:S(2)}) async-start(), calls=%async_computation.9 | async-start | bytes 3981312 | tf_op jit(solution)/shard_map/all_gather | solution.py:457
  610.4 285.0 %all-gather.15.cloned.1.call-start = ((), (), s32[]{:S(2)}) async-start(), calls=%async_computation.15 | async-start | bytes 3981312 | tf_op jit(solution)/shard_map/all_gather | solution.py:457
  655.1 282.4 %all-gather.13.cloned.1.call-start = ((), (), s32[]{:S(2)}) async-start(), calls=%async_computation.13 | async-start | bytes 3981312 | tf_op jit(solution)/shard_map/all_gather | solution.py:457
  (82 other events, 616.5 us)
Sparse Core Ops, SparseCore 0:
  10.5 78.8 all-gather.16
  91.8 26.5 all-gather.18
  347.9 68.5 reduce-scatter.8
  459.7 59.4 reduce-scatter.6
  521.9 43.7 reduce-scatter.12
  568.0 42.2 reduce-scatter.10
  612.7 42.3 reduce-scatter.16
  657.5 42.3 reduce-scatter.14
  702.3 65.8 all-reduce.11
  769.8 41.2 all-gather.10
  812.9 40.3 all-gather.8
  854.9 40.3 all-gather.14
  897.1 40.3 all-gather.12

commit v2 on v1

--- a/solution.py
+++ b/solution.py
@@ -66,8 +66,9 @@
     )(rows)
 
 
-def scatter_kernel(n, count, *refs):
+def scatter_kernel(n, count, ahead, *refs):
     parts = refs[:count]
+    refs = refs[:count] + refs[count + ahead :]
     outs = refs[count : 2 * count]
     lands = refs[2 * count : 3 * count]
     send, recv = refs[3 * count :]
@@ -95,18 +96,18 @@
         outs[i][...] = total
 
 
-def scatter_rows(n, parts, call_id):
+def scatter_rows(n, parts, call_id, ahead=()):
     count = len(parts)
     return pl.pallas_call(
-        functools.partial(scatter_kernel, n, count),
+        functools.partial(scatter_kernel, n, count, len(ahead)),
         out_shape=[jax.ShapeDtypeStruct(part.shape[1:], jnp.float32) for part in parts],
-        in_specs=[VMEM] * count,
+        in_specs=[VMEM] * count + [pl.BlockSpec(memory_space=pl.ANY)] * len(ahead),
         out_specs=[VMEM] * count,
         scratch_shapes=[pltpu.VMEM((n - 1,) + part.shape[1:], part.dtype) for part in parts]
         + [pltpu.SemaphoreType.DMA((count, n - 1)), pltpu.SemaphoreType.DMA((count, n - 1))],
         compiler_params=pltpu.CompilerParams(collective_id=call_id, has_side_effects=True),
         name="scatter_rows",
-    )(*parts)
+    )(*parts, *ahead)
 
 
 def weights_kernel(n, halved, whole, *refs):
@@ -199,13 +200,6 @@
     return (result, jnp.sum(upstream * normal, axis=0), jnp.sum(upstream, axis=0))
 
 
-def gelu_slope(values):
-    return (
-        0.5 * (1.0 + lax.erf(values * 0.7071067811865476))
-        + values * jnp.exp(-0.5 * values * values) * 0.3989422804014327
-    )
-
-
 def split_heads(packed):
     blocks = packed.reshape(packed.shape[0], 3, HEADS, HEAD_DIM)
     return (blocks[:, 0], blocks[:, 1], blocks[:, 2])
@@ -269,15 +263,13 @@
     rows = round_up(count, 16)
     layers, share = w_qkv.shape[:2]
     experts, units = expert_in.shape[1:3]
-    slots = experts * units
     padded = ((0, rows - count), (0, 0))
     live = (jnp.arange(rows, dtype=jnp.int32) // SEQ < image_count[0]).astype(jnp.float32)[:, None]
     kinds = jnp.arange(experts, dtype=jnp.int32)
     hits = (expert_ids[..., None] == kinds) & (slot_index[..., None] >= 0)
     own_mask = jnp.sum(hits.astype(jnp.float32), axis=2)
     own_mask = jnp.pad(own_mask, ((0, 0),) + padded)
-    mask_block = jnp.swapaxes(own_mask, 0, 1).reshape(rows, layers * experts)
-    mask_block = jnp.pad(mask_block, ((0, 0), (0, LANES - layers * experts)))
+    mask_block = jnp.pad(own_mask, ((0, 0), (0, 0), (0, LANES - experts)))
     smalls = jnp.concatenate(
         [
             ln_gain.reshape(2 * layers, share),
@@ -297,8 +289,8 @@
     gains = small_all[: 2 * layers].astype(jnp.float32).reshape(layers, 2, width)
     biases = small_all[2 * layers : 4 * layers].astype(jnp.float32).reshape(layers, 2, width)
     routers = small_all[4 * layers :].reshape(layers, experts, width)
-    masks = mask_all.reshape(n * rows, LANES)[:, : layers * experts].astype(jnp.float32)
-    masks = masks.reshape(n * rows, layers, experts)
+    column = jnp.arange(LANES, dtype=jnp.int32)[None, :]
+    router_tables = jnp.pad(routers, ((0, 0), (0, LANES - experts), (0, 0)))
     qkv_all = [qkv_first]
     proj_all = [proj_first]
     for layer_idx in range(1, layers):
@@ -321,27 +313,35 @@
         group_rows = gather_rows(n, second_low).reshape(n * rows, width)
         logits = lax.dot_general(
             group_rows,
-            routers[layer_idx],
+            router_tables[layer_idx],
             (((1,), (1,)), ((), ())),
             preferred_element_type=jnp.float32,
         )
-        group_probs = jax.nn.softmax(logits, axis=-1)
-        gates = group_probs * masks[:, layer_idx]
-        wide_gates = jnp.repeat(gates, units, axis=1, total_repeat_length=slots)
-        table_in = expert_in[layer_idx].reshape(slots, width)
-        table_out = expert_out[layer_idx].reshape(slots, width)
-        before = lax.dot_general(
-            group_rows, table_in, (((1,), (1,)), ((), ())), preferred_element_type=jnp.float32
-        )
-        raw_hidden = jax.nn.gelu(before, approximate=False)
-        hidden = raw_hidden.astype(jnp.bfloat16)
-        scaled_hidden = (raw_hidden * wide_gates).astype(jnp.bfloat16)
-        partial_rows = jnp.dot(scaled_hidden, table_out, preferred_element_type=jnp.float32)
+        group_probs = jax.nn.softmax(jnp.where(column < experts, logits, -jnp.inf), axis=-1)
+        gates = group_probs * mask_all[:, layer_idx].reshape(n * rows, LANES).astype(jnp.float32)
+        kept = []
+        partial_rows = None
+        for e in range(experts):
+            table_in = expert_in[layer_idx, e]
+            table_out = expert_out[layer_idx, e]
+            before = lax.dot_general(
+                group_rows, table_in, (((1,), (1,)), ((), ())), preferred_element_type=jnp.float32
+            )
+            share_below = 0.5 * (1.0 + lax.erf(before * 0.7071067811865476))
+            raw_hidden = before * share_below
+            bell = jnp.exp(-0.5 * before * before) * 0.3989422804014327
+            slope = (share_below + before * bell).astype(jnp.bfloat16)
+            hidden = raw_hidden.astype(jnp.bfloat16)
+            scaled_hidden = (raw_hidden * gates[:, e : e + 1]).astype(jnp.bfloat16)
+            hidden, scaled_hidden, slope = lax.optimization_barrier((hidden, scaled_hidden, slope))
+            kept.append((hidden, scaled_hidden, slope, table_in, table_out))
+            term = jnp.dot(scaled_hidden, table_out, preferred_element_type=jnp.float32)
+            partial_rows = term if partial_rows is None else partial_rows + term
         (combined,) = scatter_rows(
             n, [partial_rows.astype(jnp.bfloat16).reshape(n, rows, width)], 1
         )
         me = lax.axis_index("shard")
-        probs = lax.dynamic_slice_in_dim(group_probs, me * rows, rows, axis=0)
+        probs = lax.dynamic_slice_in_dim(group_probs, me * rows, rows, axis=0)[:, :experts]
         saved.append(
             (
                 first_normal,
@@ -354,13 +354,9 @@
                 second_scaled,
                 second_low,
                 probs,
-                wide_gates,
+                gates,
                 group_rows,
-                before,
-                hidden,
-                scaled_hidden,
-                table_in,
-                table_out,
+                kept,
             )
         )
         state = after + combined
@@ -380,42 +376,61 @@
             second_scaled,
             second_low,
             probs,
-            wide_gates,
+            gates,
             group_rows,
-            before,
-            hidden,
-            scaled_hidden,
-            table_in,
-            table_out,
+            kept,
         ) = saved[layer_idx]
         gain = gains[layer_idx]
         group_grad = gather_rows(n, grad_state.astype(jnp.bfloat16)).reshape(n * rows, width)
-        ungated = lax.dot_general(
-            group_grad, table_out, (((1,), (1,)), ((), ())), preferred_element_type=jnp.float32
-        )
-        gate_terms = jnp.sum(
-            (ungated * hidden.astype(jnp.float32)).reshape(n, rows, experts, units), axis=-1
-        )
-        gate_terms = jnp.pad(
-            jnp.swapaxes(gate_terms, 1, 2),
-            ((0, 0), (0, round_up(experts, 8) - experts), (0, round_up(rows, LANES) - rows)),
-        )
-        grad_before = (ungated * wide_gates * gelu_slope(before)).astype(jnp.bfloat16)
-        row_terms = jnp.dot(grad_before, table_in, preferred_element_type=jnp.float32)
+        gate_terms = jnp.zeros((n * rows, LANES), jnp.float32)
+        row_terms = None
+        pairs = []
+        for e in range(experts):
+            hidden, scaled_hidden, slope, table_in, table_out = kept[e]
+            ungated = lax.dot_general(
+                group_grad, table_out, (((1,), (1,)), ((), ())), preferred_element_type=jnp.float32
+            )
+            agreed = jnp.sum(ungated * hidden.astype(jnp.float32), axis=-1, keepdims=True)
+            coarse = lax.reduce_precision(agreed, 8, 7)
+            gate_terms = jnp.where(column == e, coarse, gate_terms)
+            gate_terms = jnp.where(column == experts + e, agreed - coarse, gate_terms)
+            grad_before = (ungated * gates[:, e : e + 1] * slope.astype(jnp.float32)).astype(
+                jnp.bfloat16
+            )
+            term = jnp.dot(grad_before, table_in, preferred_element_type=jnp.float32)
+            row_terms = term if row_terms is None else row_terms + term
+            pairs.append(((grad_before, group_rows), (scaled_hidden, group_grad)))
+        sums = [
+            jnp.concatenate(
+                [
+                    lax.dot_general(
+                        pair[which][0],
+                        pair[which][1],
+                        (((0,), (0,)), ((), ())),
+                        preferred_element_type=jnp.float32,
+                    ).astype(jnp.bfloat16)
+                    for pair in pairs
+                ]
+            )
+            for which in range(2)
+        ]
+        ahead = list(sums)
+        if layer_idx + 1 < layers:
+            ahead += expert_lists[layer_idx + 1]
         grad_rows, grad_gates = scatter_rows(
-            n, [row_terms.astype(jnp.bfloat16).reshape(n, rows, width), gate_terms], 2
-        )
-        grad_out = lax.dot_general(
-            scaled_hidden, group_grad, (((0,), (0,)), ((), ())), preferred_element_type=jnp.float32
-        )
-        grad_in = lax.dot_general(
-            grad_before, group_rows, (((0,), (0,)), ((), ())), preferred_element_type=jnp.float32
+            n,
+            [
+                row_terms.astype(jnp.bfloat16).reshape(n, rows, width),
+                gate_terms.astype(jnp.bfloat16).reshape(n, rows, LANES),
+            ],
+            2 if layer_idx + 1 == layers else 4,
+            ahead,
         )
         expert_lists[layer_idx] = [
-            lax.psum_scatter(term.astype(jnp.bfloat16), "replica", scatter_dimension=0, tiled=True)
-            for term in (grad_in, grad_out)
+            lax.psum_scatter(term, "replica", scatter_dimension=0, tiled=True) for term in sums
         ]
-        grad_probs = grad_gates[:experts, :rows].T * own_mask[layer_idx]
+        grad_gates = grad_gates[:, :experts] + grad_gates[:, experts : 2 * experts]
+        grad_probs = grad_gates * own_mask[layer_idx]
         grad_logits = probs * (grad_probs - jnp.sum(probs * grad_probs, axis=-1, keepdims=True))
         router_wide = routers[layer_idx].astype(jnp.float32)
         grad_router = jnp.dot(second_low.astype(jnp.float32).T, grad_logits, precision=precise)

time: 964 us -> 824 us (0.85)
  local copies, waits for them, and re-layouts: 103 us -> 35.5 us
  waiting for transfers between devices: 393 us -> 330 us
  matrix products: 171 us -> 146 us
  Pallas kernels: 204 us -> 219 us
    reduce_scatter x4, waiting for transfers between devices: 180 us -> 16.8 us  [body(): lax.psum_scatter(term, 'replica', scatter_dimension=0, tiled=True)]
    reduce_scatter x2, waiting for transfers between devices: 18.9 us -> 92.8 us  [body(): dense = lax.psum_scatter(dense, 'shard', scatter_dimension=0, tiled=True)]
    gather x4 -> x0, local copies, waits for them, and re-layouts: 32.9 us -> none  [body(): wide_gates = jnp.repeat(gates, units, axis=1, total_repeat_length=slots)]
    reshape x5 -> x1, local copies, waits for them, and re-layouts: 25.9 us -> 0.09 us  [body(): routers = small_all[4 * layers:].reshape(layers, experts, width)]
    dot_general x2 -> x6, matrix products: 40.9 us -> 15.4 us  [body(): lax.dot_general(group_grad, table_out, (((1,), (1,)), ((), ())), preferre...]
    pallas_call x4, Pallas kernels: 68.9 us -> 93.2 us  [scatter_rows(): pl.pallas_call(functools.partial(scatter_kernel, n, count, len(ahead)), o...]
    psum x1, waiting for transfers between devices: 40.6 us -> 59.4 us  [body(): dense_lists[layer_idx] = lax.psum(dense, 'replica').astype(jnp.float32)]
    pallas_call x4, Pallas kernels: 88.2 us -> 76.6 us  [gather_rows(): pl.pallas_call(functools.partial(gather_kernel, n), out_shape=jax.ShapeDt...]
  transfers between devices with their start and end apart: 13 -> 13, of which waited for: 10 -> 8; matrix products, arithmetic and copies ran while one was open for 22% -> 23% of each run, Pallas kernels for 18% -> 25%
where the time goes in v2:
time: 824 us; the launch traced here: 816 us
  waiting for transfers between devices  330 us (40%)
  Pallas kernels  219 us (27%)
  matrix products  146 us (18%)
  other arithmetic  67.6 us (8%)
  local copies, waits for them, and re-layouts  35.5 us (4%)
  between operations  17.2 us (2%)
    all_gather x4, waiting for transfers between devices, body(): lax.all_gather(item[which], 'replica', axis=0, tiled=True)  159 us
    pallas_call x4, Pallas kernels, scatter_rows(): pl.pallas_call(functools.partial(scatter_kernel, n, count, len(ahead)), o...  93.2 us
    reduce_scatter x2, waiting for transfers between devices, body(): dense = lax.psum_scatter(dense, 'shard', scatter_dimension=0, tiled=True)  92.8 us
    pallas_call x4, Pallas kernels, gather_rows(): pl.pallas_call(functools.partial(gather_kernel, n), out_shape=jax.ShapeDt...  76.6 us
    psum x1, waiting for transfers between devices, body(): dense_lists[layer_idx] = lax.psum(dense, 'replica').astype(jnp.float32)  59.4 us
    pallas_call x1, Pallas kernels, gather_weights(): pl.pallas_call(functools.partial(weights_kernel, n, len(halved), len(whol...  49.6 us
    dot_general x6, matrix products, body(): lax.dot_general(group_rows, table_in, (((1,), (1,)), ((), ())), preferred...  27 us
    dot_general x6, matrix products, body(): term = jnp.dot(grad_before, table_in, preferred_element_type=jnp.float32)  22.1 us
  transfers between devices with their start and end apart: 13, of which 8 were waited for; matrix products, arithmetic and copies ran while one was open for 23% of the time, Pallas kernels for 25%

profile of v2, /device:TPU:0, one launch (start us, length us, event | category | flops | bytes accessed | tf_op | source)
XLA Modules:
  0.0 815.9 jit_solution(14291076771109443252)
XLA Ops:
  12.7 49.6 %gather_weights.1 = (bf16[4,2,96,2304]{3,2,1,0:T(8,128)(2,1)}, bf16[4,2,96,768]{3,2,1,0:T(8,128)(2,1)}, bf16[4,16,256]{2,1,0:T(8,128)(2,1)}, bf16[4,2,208,128]{3,2,1,0:T(8,128)(2,1)}) custom-call(bf16[2,96,2304]{2,1,0:T(8,128)(2,1)} %bitcast.320, bf16[2,96,768]{2,1,0:T(8,128)(2,1)} %bitcast.362, bf16[16,256]{1,0:T(8,128)(2,1)} %fusion.155.refs_2_, ...), custom_call_target="tpu_custom_call" | custom-call | tf_op jit(solution)/shard_map/gather_weights/pallas_call | solution.py:170
  72.0 22.2 %gather_rows.4 = bf16[4,208,768]{2,1,0:T(8,128)(2,1)} custom-call(bf16[208,768]{1,0:T(8,128)(2,1)} %add_convert_fusion.6.x_ref), custom_call_target="tpu_custom_call" | custom-call | tf_op jit(solution)/shard_map/gather_rows/pallas_call | solution.py:58
  94.3 6.0 fusion.11
  100.3 4.9 fusion.16
  105.2 5.5 fusion.21
  130.1 19.5 %scatter_rows.4 = f32[208,768]{1,0:T(8,128)} custom-call(bf16[4,208,768]{2,1,0:T(8,128)(2,1)} %bitcast.312), custom_call_target="tpu_custom_call" | custom-call | tf_op jit(solution)/shard_map/scatter_rows/pallas_call | solution.py:101
  152.9 18.3 %gather_rows.6 = bf16[4,208,768]{2,1,0:T(8,128)(2,1)} custom-call(bf16[208,768]{1,0:T(8,128)(2,1)} %fusion.121.x_ref), custom_call_target="tpu_custom_call" | custom-call | tf_op jit(solution)/shard_map/gather_rows/pallas_call | solution.py:58
  184.4 18.4 %gather_rows.5 = bf16[4,208,768]{2,1,0:T(8,128)(2,1)} custom-call(bf16[208,768]{1,0:T(8,128)(2,1)} %add_convert_fusion.4.x_ref), custom_call_target="tpu_custom_call" | custom-call | tf_op jit(solution)/shard_map/gather_rows/pallas_call | solution.py:58
  251.0 5.5 add_convert_fusion.1
  258.6 20.1 %scatter_rows.6 = (f32[208,768]{1,0:T(8,128)}, f32[208,128]{1,0:T(8,128)}) custom-call(bf16[4,208,768]{2,1,0:T(8,128)(2,1)} %bitcast.313, bf16[4,208,128]{2,1,0:T(8,128)(2,1)} %select_convert_fusion.1.refs_1_, bf16[2304,768]{1,0:T(8,128)(2,1)} %pad_maximum_fusion.refs_2_, bf16[2304,768]{1,0:T(8,128)(2,1)} %pad_maximum_fusion.1.refs_3_), custom_call_target="tpu_custom_call" | custom-call | tf_op jit(solution)/shard_map/scatter_rows/pallas_call | solution.py:101
  297.0 17.6 %gather_rows.7 = bf16[4,208,768]{2,1,0:T(8,128)(2,1)} custom-call(bf16[208,768]{1,0:T(8,128)(2,1)} %get-tuple-element.139.x_ref), custom_call_target="tpu_custom_call" | custom-call | tf_op jit(solution)/shard_map/gather_rows/pallas_call | solution.py:58
  314.6 4.2 multiply_reduce_fusion.3
  361.7 20.3 %scatter_rows.7 = (f32[208,768]{1,0:T(8,128)}, f32[208,128]{1,0:T(8,128)}) custom-call(bf16[4,208,768]{2,1,0:T(8,128)(2,1)} %bitcast.310, bf16[4,208,128]{2,1,0:T(8,128)(2,1)} %select_convert_fusion.refs_1_, bf16[2304,768]{1,0:T(8,128)(2,1)} %pad_maximum_fusion.2.refs_2_, bf16[2304,768]{1,0:T(8,128)(2,1)} %pad_maximum_fusion.3.refs_3_, ...), custom_call_target="tpu_custom_call" | custom-call | tf_op jit(solution)/shard_map/scatter_rows/pallas_call | solution.py:101
  405.7 16.7 %reduce-scatter.17.cloned.1.call-done = bf16[288,768]{1,0:T(8,128)(2,1)} async-done(((bf16[2304,768]{1,0:T(8,128)(2,1)}), bf16[288,768]{1,0:T(8,128)(2,1)}) %reduce-scatter.17.cloned.1.call-update) | async-done | bytes 442384 | tf_op jit(solution)/shard_map/reduce_scatter | solution.py:430
  431.5 33.2 %scatter_rows.5 = f32[208,768]{1,0:T(8,128)} custom-call(bf16[4,208,768]{2,1,0:T(8,128)(2,1)} %bitcast.311), custom_call_target="tpu_custom_call" | custom-call | tf_op jit(solution)/shard_map/scatter_rows/pallas_call | solution.py:101
  466.6 30.4 %reduce-scatter.13.cloned.1.call-done = bf16[192,3200]{1,0:T(8,128)(2,1)} async-done(((bf16[768,3200]{1,0:T(8,128)(2,1)}), bf16[192,3200]{1,0:T(8,128)(2,1)}) %reduce-scatter.13.cloned.1.call-update) | async-done | bytes 1228816 | tf_op jit(solution)/shard_map/reduce_scatter | solution.py:465
  497.0 62.4 %reduce-scatter.11.cloned.1.call-done = bf16[192,3200]{1,0:T(8,128)(2,1)} async-done(((bf16[768,3200]{1,0:T(8,128)(2,1)}), bf16[192,3200]{1,0:T(8,128)(2,1)}) %reduce-scatter.11.cloned.1.call-update) | async-done | bytes 1228816 | tf_op jit(solution)/shard_map/reduce_scatter | solution.py:465
  560.4 42.1 %all-gather.11.cloned.1.call-done = bf16[2304,768]{1,0:T(8,128)(2,1)} async-done(((bf16[288,768]{1,0:T(8,128)(2,1)}), bf16[2304,768]{1,0:T(8,128)(2,1)}) %all-gather.11.cloned.1.call-update) | async-done | bytes 3538960 | tf_op jit(solution)/shard_map/all_gather | solution.py:472
  602.6 41.9 %all-gather.9.cloned.1.call-done = bf16[2304,768]{1,0:T(8,128)(2,1)} async-done(((bf16[288,768]{1,0:T(8,128)(2,1)}), bf16[2304,768]{1,0:T(8,128)(2,1)}) %all-gather.9.cloned.1.call-update) | async-done | bytes 3538960 | tf_op jit(solution)/shard_map/all_gather | solution.py:472
  644.5 9.3 %maximum_convert_fusion = f32[2,3,768,768]{3,2,1,0:T(8,128)} fusion(bf16[1,3,768,768]{3,2,1,0:T(8,128)(2,1)} %bitcast.321, bf16[1,3,768,768]{3,2,1,0:T(8,128)(2,1)} %bitcast.323), kind=kLoop, calls=%fused_computation.3 | loop fusion | flops 7077888 | bytes 21233664 | tf_op jit(solution)/shard_map/stack | solution.py:470
  653.8 32.8 %all-gather.15.cloned.1.call-done = bf16[2304,768]{1,0:T(8,128)(2,1)} async-done(((bf16[288,768]{1,0:T(8,128)(2,1)}), bf16[2304,768]{1,0:T(8,128)(2,1)}) %all-gather.15.cloned.1.call-update) | async-done | bytes 3538960 | tf_op jit(solution)/shard_map/all_gather | solution.py:472
  686.5 41.9 %all-gather.13.cloned.1.call-done = bf16[2304,768]{1,0:T(8,128)(2,1)} async-done(((bf16[288,768]{1,0:T(8,128)(2,1)}), bf16[2304,768]{1,0:T(8,128)(2,1)}) %all-gather.13.cloned.1.call-update) | async-done | bytes 3538960 | tf_op jit(solution)/shard_map/all_gather | solution.py:472
  728.5 9.3 %maximum_convert_fusion.1 = f32[2,3,768,768]{3,2,1,0:T(8,128)} fusion(bf16[1,3,768,768]{3,2,1,0:T(8,128)(2,1)} %bitcast.322, bf16[1,3,768,768]{3,2,1,0:T(8,128)(2,1)} %bitcast.324), kind=kLoop, calls=%fused_computation.4 | loop fusion | flops 7077888 | bytes 21233664 | tf_op jit(solution)/shard_map/stack | solution.py:470
  737.7 59.4 %all-reduce.11.cloned.1.call-done = (bf16[1,192,3200]{2,1,0:T(8,128)(2,1)}, bf16[1,192,3200]{2,1,0:T(8,128)(2,1)}) async-done(((bf16[1,192,3200]{2,1,0:T(8,128)(2,1)}, bf16[1,192,3200]{2,1,0:T(8,128)(2,1)}), (bf16[1,192,3200]{2,1,0:T(8,128)(2,1)}, bf16[1,192,3200]{2,1,0:T(8,128)(2,1)})) %all-reduce.11.cloned.1.call-update) | async-done | bytes 2457616 | tf_op jit(solution)/shard_map/psum | solution.py:466
  (518 shorter events, 207.0 us)
Async XLA Ops:
  7.2 164.1 %all-gather.17.cloned.1.call-start = ((), (), s32[]{:S(2)}) async-start(), calls=%async_computation.16 | async-start | bytes 4423680 | tf_op jit(solution)/shard_map/all_gather | solution.py:297
  10.1 53.3 %copy-start.19 = (bf16[197,768]{1,0:T(8,128)(2,1)S(1)}, bf16[197,768]{1,0:T(8,128)(2,1)}, u32[]{:S(2)}) copy-start(bf16[197,768]{1,0:T(8,128)(2,1)} %param.12) | copy-start | bytes 907780
  10.1 170.6 %all-gather.19.cloned.1.call-start = ((), (), s32[]{:S(2)}) async-start(), calls=%async_computation.17 | async-start | bytes 1474560 | tf_op jit(solution)/shard_map/all_gather | solution.py:298
  11.1 350.6 %reduce-scatter.7.cloned.1.call-start = ((), (), s32[]{:S(2)}) async-start(), calls=%async_computation.6 | async-start | bytes 3981312 | tf_op jit(solution)/shard_map/reduce_scatter | solution.py:430
  69.7 24.6 %copy-start.37 = (bf16[12,64,208]{2,1,0:T(8,128)(2,1)}, bf16[12,64,208]{2,1,0:T(8,128)(2,1)S(1)}, u32[]{:S(2)}) copy-start(bf16[12,64,208]{2,1,0:T(8,128)(2,1)S(1)} %convolution_convert_fusion.20) | copy-start | bytes 958468
  70.9 78.8 %copy-start.2 = (f32[208,768]{1,0:T(8,128)}, f32[208,768]{1,0:T(8,128)S(1)}, u32[]{:S(2)}) copy-start(f32[208,768]{1,0:T(8,128)S(1)} %get-tuple-element.214) | copy-start | bytes 1916932
  70.9 29.5 %copy-start.78 = (f32[208]{0:T(256)}, f32[208]{0:T(256)S(1)}, u32[]{:S(2)}) copy-start(f32[208]{0:T(256)S(1)} %broadcast_multiply_fusion.11) | copy-start | bytes 2500
  71.1 29.2 %copy-start.90 = (f32[208]{0:T(256)}, f32[208]{0:T(256)S(1)}, u32[]{:S(2)}) copy-start(f32[208]{0:T(256)S(1)} %add_rsqrt_fusion.2) | copy-start | bytes 2500
  151.5 22.8 %copy-start.102 = (f32[208]{0:T(256)}, f32[208]{0:T(256)S(1)}, u32[]{:S(2)}) copy-start(f32[208]{0:T(256)S(1)} %compare_convert_fusion) | copy-start | bytes 2500
  183.5 25.0 %copy-start.92 = (f32[208]{0:T(256)}, f32[208]{0:T(256)S(1)}, u32[]{:S(2)}) copy-start(f32[208]{0:T(256)S(1)} %add_rsqrt_fusion) | copy-start | bytes 2500
  233.1 128.6 %reduce-scatter.9.cloned.1.call-start = ((), (), s32[]{:S(2)}) async-start(), calls=%async_computation.7 | async-start | bytes 3981312 | tf_op jit(solution)/shard_map/reduce_scatter | solution.py:430
  256.6 147.8 %reduce-scatter.15.cloned.1.call-start = ((), (), s32[]{:S(2)}) async-start(), calls=%async_computation.10 | async-start | bytes 3981312 | tf_op jit(solution)/shard_map/reduce_scatter | solution.py:430
  334.0 88.4 %reduce-scatter.17.cloned.1.call-start = ((), (), s32[]{:S(2)}) async-start(), calls=%async_computation.13 | async-start | bytes 3981312 | tf_op jit(solution)/shard_map/reduce_scatter | solution.py:430
  343.4 153.7 %reduce-scatter.13.cloned.1.call-start = ((), (), s32[]{:S(2)}) async-start(), calls=%async_computation.9 | async-start | bytes 6144000 | tf_op jit(solution)/shard_map/reduce_scatter | solution.py:465
  350.3 209.1 %reduce-scatter.11.cloned.1.call-start = ((), (), s32[]{:S(2)}) async-start(), calls=%async_computation.8 | async-start | bytes 6144000 | tf_op jit(solution)/shard_map/reduce_scatter | solution.py:465
  403.6 198.9 %all-gather.11.cloned.1.call-start = ((), (), s32[]{:S(2)}) async-start(), calls=%async_computation.12 | async-start | bytes 3981312 | tf_op jit(solution)/shard_map/all_gather | solution.py:472
  404.3 240.1 %all-gather.9.cloned.1.call-start = ((), (), s32[]{:S(2)}) async-start(), calls=%async_computation.11 | async-start | bytes 3981312 | tf_op jit(solution)/shard_map/all_gather | solution.py:472
  404.9 281.6 %all-gather.15.cloned.1.call-start = ((), (), s32[]{:S(2)}) async-start(), calls=%async_computation.15 | async-start | bytes 3981312 | tf_op jit(solution)/shard_map/all_gather | solution.py:472
  405.7 322.8 %all-gather.13.cloned.1.call-start = ((), (), s32[]{:S(2)}) async-start(), calls=%async_computation.14 | async-start | bytes 3981312 | tf_op jit(solution)/shard_map/all_gather | solution.py:472
  422.5 374.7 %all-reduce.11.cloned.1.call-start = ((), (), s32[]{:S(2)}) async-start(), calls=%async_computation.18 | async-start | bytes 4915200 | tf_op jit(solution)/shard_map/psum | solution.py:466
  427.9 36.8 %copy-start.6 = (f32[208,768]{1,0:T(8,128)S(1)}, f32[208,768]{1,0:T(8,128)}, u32[]{:S(2)}) copy-start(f32[208,768]{1,0:T(8,128)} %copy-done.4) | copy-start | bytes 1916932
  427.9 36.8 %copy-start.104 = (f32[208]{0:T(256)S(1)}, f32[208]{0:T(256)}, u32[]{:S(2)}) copy-start(f32[208]{0:T(256)} %copy-done.102) | copy-start | bytes 2500
  431.5 127.9 %copy-start.66 = (f32[208,768]{1,0:T(8,128)S(1)}, f32[208,768]{1,0:T(8,128)}, u32[]{:S(2)}) copy-start(f32[208,768]{1,0:T(8,128)} %get-tuple-element.189) | copy-start | bytes 1916932
  431.5 127.9 %copy-start.67 = (f32[208,768]{1,0:T(8,128)S(1)}, f32[208,768]{1,0:T(8,128)}, u32[]{:S(2)}) copy-start(f32[208,768]{1,0:T(8,128)} %get-tuple-element.194) | copy-start | bytes 1916932
  (134 other events, 633.2 us)
Sparse Core Ops, SparseCore 0:
  10.5 78.9 all-gather.16
  91.9 26.5 all-gather.18
  233.2 43.7 reduce-scatter.6
  279.9 42.2 reduce-scatter.8
  334.1 43.6 reduce-scatter.14
  380.1 42.3 reduce-scatter.16
  426.1 70.9 reduce-scatter.12
  500.6 58.7 reduce-scatter.10
  561.0 41.4 all-gather.10
  604.0 40.3 all-gather.8
  646.1 40.3 all-gather.14
  688.0 40.3 all-gather.12
  730.9 66.1 all-reduce.10

commit v3 on v2

--- a/solution.py
+++ b/solution.py
@@ -105,7 +105,9 @@
         out_specs=[VMEM] * count,
         scratch_shapes=[pltpu.VMEM((n - 1,) + part.shape[1:], part.dtype) for part in parts]
         + [pltpu.SemaphoreType.DMA((count, n - 1)), pltpu.SemaphoreType.DMA((count, n - 1))],
-        compiler_params=pltpu.CompilerParams(collective_id=call_id, has_side_effects=True),
+        compiler_params=pltpu.CompilerParams(
+            collective_id=call_id, has_side_effects=True, vmem_limit_bytes=40 * 1024 * 1024
+        ),
         name="scatter_rows",
     )(*parts, *ahead)
 
@@ -462,7 +464,8 @@
             ],
             axis=1,
         )
-        dense = lax.psum_scatter(dense, "shard", scatter_dimension=0, tiled=True)
+        (dense,) = scatter_rows(n, [dense.reshape(n, share, dense.shape[1])], 5)
+        dense = dense.astype(jnp.bfloat16)
         dense_lists[layer_idx] = lax.psum(dense, "replica").astype(jnp.float32)
     expert_grads = []
     for which in range(2):

time: 824 us -> 779 us (0.945)
  waiting for transfers between devices: 330 us -> 195 us
  Pallas kernels: 219 us -> 302 us
  local copies, waits for them, and re-layouts: 35.5 us -> 50.2 us
    reduce_scatter x2 -> x0, waiting for transfers between devices: 92.8 us -> none  [body(): dense = lax.psum_scatter(dense, 'shard', scatter_dimension=0, tiled=True)]
    pallas_call x4 -> x6, Pallas kernels: 93.2 us -> 179 us  [scatter_rows(): pl.pallas_call(functools.partial(scatter_kernel, n, count, len(ahead)), o...]
    psum x1, waiting for transfers between devices: 59.4 us -> 38.9 us  [body(): dense_lists[layer_idx] = lax.psum(dense, 'replica').astype(jnp.float32)]
    reduce_scatter x4, waiting for transfers between devices: 16.8 us -> 0.04 us  [body(): lax.psum_scatter(term, 'replica', scatter_dimension=0, tiled=True)]
    unnamed x290 -> x338, local copies, waits for them, and re-layouts: 16.5 us -> 29.6 us
  transfers between devices with their start and end apart: 13 -> 11, of which waited for: 8 -> 5; matrix products, arithmetic and copies ran while one was open for 23% -> 24% of each run, Pallas kernels for 25% -> 37%
where the time goes in v3:
time: 779 us; the launch traced here: 771 us
  Pallas kernels  302 us (39%)
  waiting for transfers between devices  195 us (25%)
  matrix products  141 us (18%)
  other arithmetic  64.8 us (8%)
  local copies, waits for them, and re-layouts  50.2 us (6%)
  between operations  17.5 us (2%)
    pallas_call x6, Pallas kernels, scatter_rows(): pl.pallas_call(functools.partial(scatter_kernel, n, count, len(ahead)), o...  179 us
    all_gather x4, waiting for transfers between devices, body(): lax.all_gather(item[which], 'replica', axis=0, tiled=True)  153 us
    pallas_call x4, Pallas kernels, gather_rows(): pl.pallas_call(functools.partial(gather_kernel, n), out_shape=jax.ShapeDt...  73.4 us
    pallas_call x1, Pallas kernels, gather_weights(): pl.pallas_call(functools.partial(weights_kernel, n, len(halved), len(whol...  49.6 us
    psum x1, waiting for transfers between devices, body(): dense_lists[layer_idx] = lax.psum(dense, 'replica').astype(jnp.float32)  38.9 us
    unnamed x338, local copies, waits for them, and re-layouts  29.6 us
    dot_general x6, matrix products, body(): lax.dot_general(group_rows, table_in, (((1,), (1,)), ((), ())), preferred...  26.4 us
    dot_general x6, matrix products, body(): term = jnp.dot(grad_before, table_in, preferred_element_type=jnp.float32)  22.5 us
  transfers between devices with their start and end apart: 11, of which 5 were waited for; matrix products, arithmetic and copies ran while one was open for 24% of the time, Pallas kernels for 37%

profile of v3, /device:TPU:0, one launch (start us, length us, event | category | flops | bytes accessed | tf_op | source)
XLA Modules:
  0.0 771.1 jit_solution(15651228686135769962)
XLA Ops:
  12.8 49.6 %gather_weights.1 = (bf16[4,2,96,2304]{3,2,1,0:T(8,128)(2,1)}, bf16[4,2,96,768]{3,2,1,0:T(8,128)(2,1)}, bf16[4,16,256]{2,1,0:T(8,128)(2,1)}, bf16[4,2,208,128]{3,2,1,0:T(8,128)(2,1)}) custom-call(bf16[2,96,2304]{2,1,0:T(8,128)(2,1)} %bitcast.326, bf16[2,96,768]{2,1,0:T(8,128)(2,1)} %bitcast.366, bf16[16,256]{1,0:T(8,128)(2,1)} %fusion.155.refs_2_, ...), custom_call_target="tpu_custom_call" | custom-call | tf_op jit(solution)/shard_map/gather_weights/pallas_call | solution.py:172
  74.4 19.8 %gather_rows.4 = bf16[4,208,768]{2,1,0:T(8,128)(2,1)} custom-call(bf16[208,768]{1,0:T(8,128)(2,1)} %add_convert_fusion.6.x_ref), custom_call_target="tpu_custom_call" | custom-call | tf_op jit(solution)/shard_map/gather_rows/pallas_call | solution.py:58
  94.3 6.1 fusion.11
  100.4 4.9 fusion.16
  105.3 4.8 fusion.21
  130.8 17.5 %scatter_rows.6 = f32[208,768]{1,0:T(8,128)S(1)} custom-call(bf16[4,208,768]{2,1,0:T(8,128)(2,1)S(1)} %bitcast.308), custom_call_target="tpu_custom_call" | custom-call | tf_op jit(solution)/shard_map/scatter_rows/pallas_call | solution.py:101
  151.0 18.0 %gather_rows.6 = bf16[4,208,768]{2,1,0:T(8,128)(2,1)} custom-call(bf16[208,768]{1,0:T(8,128)(2,1)} %fusion.121.x_ref), custom_call_target="tpu_custom_call" | custom-call | tf_op jit(solution)/shard_map/gather_rows/pallas_call | solution.py:58
  181.8 18.1 %gather_rows.5 = bf16[4,208,768]{2,1,0:T(8,128)(2,1)} custom-call(bf16[208,768]{1,0:T(8,128)(2,1)} %add_convert_fusion.4.x_ref), custom_call_target="tpu_custom_call" | custom-call | tf_op jit(solution)/shard_map/gather_rows/pallas_call | solution.py:58
  250.2 4.8 add_convert_fusion.1
  260.7 18.0 %scatter_rows.8 = (f32[208,768]{1,0:T(8,128)S(1)}, f32[208,128]{1,0:T(8,128)S(1)}) custom-call(bf16[4,208,768]{2,1,0:T(8,128)(2,1)S(1)} %bitcast.309, bf16[4,208,128]{2,1,0:T(8,128)(2,1)S(1)} %select_convert_fusion.1.refs_1_, bf16[2304,768]{1,0:T(8,128)(2,1)S(1)} %copy-done, bf16[2304,768]{1,0:T(8,128)(2,1)S(1)} %copy-done.2), custom_call_target="tpu_custom_call" | custom-call | tf_op jit(solution)/shard_map/scatter_rows/pallas_call | solution.py:101
  292.0 17.5 %gather_rows.7 = bf16[4,208,768]{2,1,0:T(8,128)(2,1)} custom-call(bf16[208,768]{1,0:T(8,128)(2,1)} %get-tuple-element.139.x_ref), custom_call_target="tpu_custom_call" | custom-call | tf_op jit(solution)/shard_map/gather_rows/pallas_call | solution.py:58
  342.7 4.0 fusion.82
  351.9 4.8 add_convert_fusion
  363.0 55.1 %scatter_rows.11 = f32[192,3200]{1,0:T(8,128)S(1)} custom-call(bf16[4,192,3200]{2,1,0:T(8,128)(2,1)S(1)} %bitcast.304), custom_call_target="tpu_custom_call" | custom-call | tf_op jit(solution)/shard_map/scatter_rows/pallas_call | solution.py:101
  426.8 18.0 %scatter_rows.9 = (f32[208,768]{1,0:T(8,128)S(1)}, f32[208,128]{1,0:T(8,128)S(1)}) custom-call(bf16[4,208,768]{2,1,0:T(8,128)(2,1)S(1)} %bitcast.306, bf16[4,208,128]{2,1,0:T(8,128)(2,1)S(1)} %copy-done.8, bf16[2304,768]{1,0:T(8,128)(2,1)S(1)} %copy-done.1, bf16[2304,768]{1,0:T(8,128)(2,1)S(1)} %copy-done.3, bf16[288,768]{1,0:T(8,128)(2,1)S(1)} %copy-done.6, ...), custom_call_target="tpu_custom_call" | custom-call | tf_op jit(solution)/shard_map/scatter_rows/pallas_call | solution.py:101
  462.4 55.0 %scatter_rows.10 = f32[192,3200]{1,0:T(8,128)S(1)} custom-call(bf16[4,192,3200]{2,1,0:T(8,128)(2,1)S(1)} %bitcast.305), custom_call_target="tpu_custom_call" | custom-call | tf_op jit(solution)/shard_map/scatter_rows/pallas_call | solution.py:101
  529.1 15.6 %scatter_rows.7 = f32[208,768]{1,0:T(8,128)S(1)} custom-call(bf16[4,208,768]{2,1,0:T(8,128)(2,1)S(1)} %bitcast.307), custom_call_target="tpu_custom_call" | custom-call | tf_op jit(solution)/shard_map/scatter_rows/pallas_call | solution.py:101
  546.6 38.9 %all-reduce.11.cloned.1.call-done = (bf16[1,192,3200]{2,1,0:T(8,128)(2,1)}, bf16[1,192,3200]{2,1,0:T(8,128)(2,1)}) async-done(((bf16[1,192,3200]{2,1,0:T(8,128)(2,1)}, bf16[1,192,3200]{2,1,0:T(8,128)(2,1)}), (bf16[1,192,3200]{2,1,0:T(8,128)(2,1)}, bf16[1,192,3200]{2,1,0:T(8,128)(2,1)})) %all-reduce.11.cloned.1.call-update) | async-done | bytes 2457616 | tf_op jit(solution)/shard_map/psum | solution.py:469
  592.4 36.1 %all-gather.11.cloned.1.call-done = bf16[2304,768]{1,0:T(8,128)(2,1)} async-done(((bf16[288,768]{1,0:T(8,128)(2,1)}), bf16[2304,768]{1,0:T(8,128)(2,1)}) %all-gather.11.cloned.1.call-update) | async-done | bytes 3538960 | tf_op jit(solution)/shard_map/all_gather | solution.py:475
  628.5 42.2 %all-gather.9.cloned.1.call-done = bf16[2304,768]{1,0:T(8,128)(2,1)} async-done(((bf16[288,768]{1,0:T(8,128)(2,1)}), bf16[2304,768]{1,0:T(8,128)(2,1)}) %all-gather.9.cloned.1.call-update) | async-done | bytes 3538960 | tf_op jit(solution)/shard_map/all_gather | solution.py:475
  670.7 9.3 %maximum_convert_fusion = f32[2,3,768,768]{3,2,1,0:T(8,128)} fusion(bf16[1,3,768,768]{3,2,1,0:T(8,128)(2,1)} %bitcast.327, bf16[1,3,768,768]{3,2,1,0:T(8,128)(2,1)} %bitcast.329), kind=kLoop, calls=%fused_computation.3 | loop fusion | flops 7077888 | bytes 21233664 | tf_op jit(solution)/shard_map/stack | solution.py:473
  679.9 32.7 %all-gather.15.cloned.1.call-done = bf16[2304,768]{1,0:T(8,128)(2,1)} async-done(((bf16[288,768]{1,0:T(8,128)(2,1)}), bf16[2304,768]{1,0:T(8,128)(2,1)}) %all-gather.15.cloned.1.call-update) | async-done | bytes 3538960 | tf_op jit(solution)/shard_map/all_gather | solution.py:475
  712.7 42.2 %all-gather.13.cloned.1.call-done = bf16[2304,768]{1,0:T(8,128)(2,1)} async-done(((bf16[288,768]{1,0:T(8,128)(2,1)}), bf16[2304,768]{1,0:T(8,128)(2,1)}) %all-gather.13.cloned.1.call-update) | async-done | bytes 3538960 | tf_op jit(solution)/shard_map/all_gather | solution.py:475
  754.8 9.3 %maximum_convert_fusion.1 = f32[2,3,768,768]{3,2,1,0:T(8,128)} fusion(bf16[1,3,768,768]{3,2,1,0:T(8,128)(2,1)} %bitcast.328, bf16[1,3,768,768]{3,2,1,0:T(8,128)(2,1)} %bitcast.330), kind=kLoop, calls=%fused_computation.4 | loop fusion | flops 7077888 | bytes 21233664 | tf_op jit(solution)/shard_map/stack | solution.py:473
  (564 shorter events, 211.7 us)
Async XLA Ops:
  7.2 161.8 %all-gather.17.cloned.1.call-start = ((), (), s32[]{:S(2)}) async-start(), calls=%async_computation.12 | async-start | bytes 4423680 | tf_op jit(solution)/shard_map/all_gather | solution.py:299
  10.1 54.4 %copy-start.33 = (bf16[197,768]{1,0:T(8,128)(2,1)S(1)}, bf16[197,768]{1,0:T(8,128)(2,1)}, u32[]{:S(2)}) copy-start(bf16[197,768]{1,0:T(8,128)(2,1)} %param.12) | copy-start | bytes 907780
  10.1 167.4 %all-gather.19.cloned.1.call-start = ((), (), s32[]{:S(2)}) async-start(), calls=%async_computation.13 | async-start | bytes 1474560 | tf_op jit(solution)/shard_map/all_gather | solution.py:300
  11.1 408.2 %reduce-scatter.5.cloned.1.call-start = ((), (), s32[]{:S(2)}) async-start(), calls=%async_computation.4 | async-start | bytes 3981312 | tf_op jit(solution)/shard_map/reduce_scatter | solution.py:432
  11.1 164.8 %copy-start.102 = (pred[208]{0:T(512)(128)(4,1)}, pred[208]{0:T(512)(128)(4,1)S(1)}, u32[]{:S(2)}) copy-start(pred[208]{0:T(512)(128)(4,1)S(1)} %iota_compare_fusion.3) | copy-start | bytes 628
  11.4 56.5 %copy-start.41 = (f32[2,197,3]{2,1,0:T(8,128)}, f32[2,197,3]{2,1,0:T(8,128)S(1)}, u32[]{:S(2)}) copy-start(f32[2,197,3]{2,1,0:T(8,128)S(1)} %copy.106) | copy-start | bytes 14188
  73.2 75.1 %copy-start.16 = (f32[208,768]{1,0:T(8,128)}, f32[208,768]{1,0:T(8,128)S(1)}, u32[]{:S(2)}) copy-start(f32[208,768]{1,0:T(8,128)S(1)} %get-tuple-element.214) | copy-start | bytes 1916932
  73.3 27.1 %copy-start.105 = (f32[208]{0:T(256)}, f32[208]{0:T(256)S(1)}, u32[]{:S(2)}) copy-start(f32[208]{0:T(256)S(1)} %broadcast_multiply_fusion.11) | copy-start | bytes 2500
  73.5 26.9 %copy-start.119 = (f32[208]{0:T(256)}, f32[208]{0:T(256)S(1)}, u32[]{:S(2)}) copy-start(f32[208]{0:T(256)S(1)} %add_rsqrt_fusion.2) | copy-start | bytes 2500
  130.8 19.9 %copy-start.128 = (f32[4,192]{1,0:T(4,128)S(1)}, f32[4,192]{1,0:T(4,128)}, u32[]{:S(2)}) copy-start(f32[4,192]{1,0:T(4,128)} %get-tuple-element.238) | copy-start | bytes 9220
  130.8 20.1 %copy-start.127 = (f32[4,192]{1,0:T(4,128)S(1)}, f32[4,192]{1,0:T(4,128)}, u32[]{:S(2)}) copy-start(f32[4,192]{1,0:T(4,128)} %get-tuple-element.239) | copy-start | bytes 9220
  148.5 29.1 %copy-start.13 = (f32[208,768]{1,0:T(8,128)}, f32[208,768]{1,0:T(8,128)S(1)}, u32[]{:S(2)}) copy-start(f32[208,768]{1,0:T(8,128)S(1)} %get-tuple-element.152) | copy-start | bytes 1916932
  148.5 24.4 %copy-start.99 = (f32[208]{0:T(256)}, f32[208]{0:T(256)S(1)}, u32[]{:S(2)}) copy-start(f32[208]{0:T(256)S(1)} %broadcast_multiply_fusion.10) | copy-start | bytes 2500
  150.6 22.3 %copy-start.109 = (f32[208]{0:T(256)}, f32[208]{0:T(256)S(1)}, u32[]{:S(2)}) copy-start(f32[208]{0:T(256)S(1)} %add_rsqrt_fusion.1) | copy-start | bytes 2500
  177.5 22.4 %copy-start.56 = (bf16[12,64,208]{2,1,0:T(8,128)(2,1)}, bf16[12,64,208]{2,1,0:T(8,128)(2,1)S(1)}, u32[]{:S(2)}) copy-start(bf16[12,64,208]{2,1,0:T(8,128)(2,1)S(1)} %convolution_convert_fusion.19) | copy-start | bytes 958468
  214.8 25.4 %copy-start.60 = (bf16[832,768]{1,0:T(8,128)(2,1)}, bf16[832,768]{1,0:T(8,128)(2,1)S(1)}, u32[]{:S(2)}) copy-start(bf16[832,768]{1,0:T(8,128)(2,1)S(1)} %get-tuple-element.43) | copy-start | bytes 3833860
  230.2 189.1 %reduce-scatter.7.cloned.1.call-start = ((), (), s32[]{:S(2)}) async-start(), calls=%async_computation.5 | async-start | bytes 3981312 | tf_op jit(solution)/shard_map/reduce_scatter | solution.py:432
  255.0 264.4 %reduce-scatter.9.cloned.1.call-start = ((), (), s32[]{:S(2)}) async-start(), calls=%async_computation.6 | async-start | bytes 3981312 | tf_op jit(solution)/shard_map/reduce_scatter | solution.py:432
  327.2 193.8 %reduce-scatter.11.cloned.1.call-start = ((), (), s32[]{:S(2)}) async-start(), calls=%async_computation.9 | async-start | bytes 3981312 | tf_op jit(solution)/shard_map/reduce_scatter | solution.py:432
  356.8 228.7 %all-reduce.11.cloned.1.call-start = ((), (), s32[]{:S(2)}) async-start(), calls=%async_computation.14 | async-start | bytes 4915200 | tf_op jit(solution)/shard_map/psum | solution.py:469
  518.6 109.9 %all-gather.11.cloned.1.call-start = ((), (), s32[]{:S(2)}) async-start(), calls=%async_computation.8 | async-start | bytes 3981312 | tf_op jit(solution)/shard_map/all_gather | solution.py:475
  519.3 151.3 %all-gather.9.cloned.1.call-start = ((), (), s32[]{:S(2)}) async-start(), calls=%async_computation.7 | async-start | bytes 3981312 | tf_op jit(solution)/shard_map/all_gather | solution.py:475
  520.1 192.6 %all-gather.15.cloned.1.call-start = ((), (), s32[]{:S(2)}) async-start(), calls=%async_computation.11 | async-start | bytes 3981312 | tf_op jit(solution)/shard_map/all_gather | solution.py:475
  520.7 234.2 %all-gather.13.cloned.1.call-start = ((), (), s32[]{:S(2)}) async-start(), calls=%async_computation.10 | async-start | bytes 3981312 | tf_op jit(solution)/shard_map/all_gather | solution.py:475
  (156 other events, 704.4 us)
Sparse Core Ops, SparseCore 0:
  10.5 70.1 all-gather.16
  83.1 28.3 all-gather.18
  230.3 43.1 reduce-scatter.4
  276.4 42.3 reduce-scatter.6
  327.3 43.1 reduce-scatter.8
  372.8 42.3 reduce-scatter.10
  518.7 66.6 all-reduce.10
  587.2 41.2 all-gather.10
  630.2 40.3 all-gather.8
  672.2 40.3 all-gather.14
  714.4 40.3 all-gather.12
